TPU v7x, 256 devices: a whole 4x4x8 slice. The times are simulated.
256 devices in a mesh: row: 8 (over z), col: 32 (over y, x, core).
Axes of the slice: x: 4, y: 4, z: 8, core: 2. Of those that a mesh axis runs over, the one named last changes fastest.
Arguments:
- tokens: bfloat16 [1024, 6144], P('row', 'col'), may hold values from -600 to 600
- norm_gain: float32 [6144], P('col'), may hold values from 0.1 to 1.9
- up_weight: bfloat16 [6144, 24576], P('row', 'col'), may hold values from -0.078125 to 0.078125
- up_bias: float32 [24576], P('col'), may hold values from -3 to 3
- cotangent: bfloat16 [1024, 24576], P('row', 'col'), may hold values from -6 to 6
Outputs:
- activated: bfloat16 [1024, 24576], P('row', 'col')
- input_grad: bfloat16 [1024, 6144], P('row', 'col')
- weight_grad: float32 [6144, 24576], P('row', 'col')
- bias_grad: float32 [24576], P('col')
- gain_grad: float32 [6144], P('col')
All inputs are finite; a program needn't handle non-finite values.
Results may differ from a plain program's by a relative error of at most 0.0055.
Values may be sent and summed in bfloat16 or wider, within the bound.
A program may use at most 128 MiB of HBM per device.

v0:
```python
import jax
import jax.numpy as jnp
from jax import lax
from jax.sharding import PartitionSpec as P

D = 6144


def gelu_exact(value):
    return jax.nn.gelu(value, approximate=False)


def body(tokens, norm_gain, up_weight, up_bias, cotangent):
    xf = tokens.astype(jnp.float32)
    total = lax.psum(jnp.sum(xf, axis=1), "col")
    mean = (total / D)[:, None]
    centred = xf - mean
    squares = lax.psum(jnp.sum(centred * centred, axis=1), "col")
    var = (squares / D)[:, None]
    rstd = lax.rsqrt(var + 1e-06)
    normed = centred * rstd
    scaled = (normed * norm_gain).astype(jnp.bfloat16)
    scaled_full = lax.all_gather(scaled, "col", axis=1, tiled=True)
    weight_full = lax.all_gather(up_weight, "row", axis=0, tiled=True)
    pre = jnp.dot(scaled_full, weight_full, preferred_element_type=jnp.float32) + up_bias
    activated = gelu_exact(pre).astype(jnp.bfloat16)
    _, back = jax.vjp(gelu_exact, pre)
    pre_grad = back(cotangent.astype(jnp.float32))[0].astype(jnp.bfloat16)
    scaled_grad = lax.psum_scatter(
        lax.dot_general(
            weight_full, pre_grad, (((1,), (1,)), ((), ())), preferred_element_type=jnp.float32
        ),
        "col",
        scatter_dimension=0,
        tiled=True,
    ).T
    grads = scaled_grad * norm_gain
    first, second = lax.psum((jnp.sum(grads, axis=1), jnp.sum(grads * normed, axis=1)), "col")
    first = (first / D)[:, None]
    second = (second / D)[:, None]
    input_grad = (rstd * (grads - first - normed * second)).astype(jnp.bfloat16)
    gain_part = jnp.sum(scaled_grad * normed, axis=0)
    grad_all = lax.all_gather(pre_grad, "row", axis=0, tiled=True)
    scaled_block = lax.all_to_all(scaled_full, "row", split_axis=1, concat_axis=0, tiled=True)
    weight_grad = lax.dot_general(
        scaled_block, grad_all, (((0,), (0,)), ((), ())), preferred_element_type=jnp.float32
    )
    bias_grad = jnp.sum(grad_all.astype(jnp.float32), axis=0)
    gain_grad = lax.psum(gain_part, "row")
    return (activated, input_grad, weight_grad, bias_grad, gain_grad)


def solution(mesh):
    in_specs = (P("row", "col"), P("col"), P("row", "col"), P("col"), P("row", "col"))
    out_specs = (P("row", "col"), P("row", "col"), P("row", "col"), P("col"), P("col"))
    return jax.shard_map(body, mesh=mesh, in_specs=in_specs, out_specs=out_specs, check_vma=False)
```

profile of v0, /device:TPU:1, one launch (start us, length us, event | category | flops | bytes accessed | tf_op | source)
XLA Modules:
  0.0 543.8 jit_solution(5755758128241584813)
XLA Ops:
  7.2 0.8 convert_reduce_fusion.1
  8.1 65.3 %psum.35 = f32[128]{0:T(128)S(1)} all-reduce(f32[128]{0:T(128)S(1)} %convert_reduce_fusion.1), channel_id=1, replica_groups=mesh['row'=8,'col'=32] {'col'}, use_global_device_ids=true, to_apply=%region_1.0 | all-reduce | flops 128 | bytes 1024 | tf_op jit(solution)/shard_map/psum | solution.py:15
  73.3 0.8 fusion.25
  74.2 65.6 %psum.36 = f32[128]{0:T(128)S(1)} all-reduce(f32[128]{0:T(128)S(1)} %fusion.25), channel_id=1, replica_groups=mesh['row'=8,'col'=32] {'col'}, use_global_device_ids=true, to_apply=%region_3.0 | all-reduce | flops 128 | bytes 1024 | tf_op jit(solution)/shard_map/psum | solution.py:18
  139.7 1.5 fusion.19
  141.3 0.0 all-gather.6.cloned.1.call-start
  141.3 0.7 all-gather.6.cloned.1.call-update
  142.1 45.9 %all-gather.4.cloned.1.call-done = bf16[128,6144]{0,1:T(8,128)(2,1)} async-done(((bf16[128,192]{0,1:T(8,128)(2,1)}), bf16[128,6144]{0,1:T(8,128)(2,1)}) %all-gather.4.cloned.1.call-update) | async-done | bytes 1572880 | tf_op jit(solution)/shard_map/all_gather | solution.py:23
  188.0 104.8 %all-gather.6.cloned.1.call-done = bf16[6144,768]{1,0:T(8,128)(2,1)} async-done(((bf16[768,768]{1,0:T(8,128)(2,1)}), bf16[6144,768]{1,0:T(8,128)(2,1)}) %all-gather.6.cloned.1.call-update) | async-done | bytes 9437200 | tf_op jit(solution)/shard_map/all_gather | solution.py:24
  292.7 7.3 %fusion.5 = (bf16[128,768]{1,0:T(8,128)(2,1)}, f32[128,768]{1,0:T(8,128)}, f32[128,768]{1,0:T(8,128)}) fusion(bf16[128,768]{1,0:T(8,128)(2,1)} %param.9, f32[768]{0:T(1024)} %param.8, bf16[128,6144]{0,1:T(8,128)(2,1)} %all-gather.4.cloned.1.call-done, bf16[6144,768]{1,0:T(8,128)(2,1)} %all-gather.6.cloned.1.call-done), kind=kOutput, calls=%fused_computation.11 | convolution fusion | flops 1215234048 | bytes 12192768 | tf_op jit(solution)/shard_map/dot_general | solution.py:25
  300.1 0.0 reduce-scatter.4.cloned.1.call-start
  300.2 6.9 %convolution_bitcast_fusion = f32[6144,128]{0,1:T(8,128)S(1)} fusion(bf16[128,768]{1,0:T(8,128)(2,1)} %get-tuple-element.20, bf16[6144,768]{1,0:T(8,128)(2,1)} %all-gather.6.cloned.1.call-done), kind=kOutput, calls=%fused_computation | convolution fusion | flops 1207959552 | bytes 12779520 | tf_op jit(solution)/shard_map/dot_general | solution.py:30
  307.0 2.4 copy.18
  309.4 1.4 copy-done
  310.9 53.0 %all_to_all.19 = bf16[128,8,768]{0,2,1:T(8,128)(2,1)S(1)} all-to-all(bf16[128,8,768]{0,2,1:T(8,128)(2,1)S(1)} %bitcast.22), channel_id=1, replica_groups=mesh['row'=8,'col'=32] {'row'}, dimensions={1} | all-to-all | bytes 3145728 | tf_op jit(solution)/shard_map/all_to_all | solution.py:44
  363.9 0.7 copy.17
  364.6 1.8 multiply_convert_fusion
  366.4 2.4 convert_reduce_fusion
  368.8 2.8 fusion.28
  371.7 80.6 %reduce-scatter.4.cloned.1.call-done = f32[192,128]{1,0:T(8,128)} async-done(((f32[6144,128]{1,0:T(8,128)}), f32[192,128]{1,0:T(8,128)}) %reduce-scatter.4.cloned.1.call-update) | async-done | bytes 98320 | tf_op jit(solution)/shard_map/reduce_scatter | solution.py:29
  452.3 1.0 fusion.24
  453.4 14.3 %psum.39 = f32[192]{0:T(256)} all-reduce(f32[192]{0:T(256)S(1)} %get-tuple-element.15), channel_id=1, replica_groups=mesh['row'=8,'col'=32] {'row'}, use_global_device_ids=true, to_apply=%region_11.0 | all-reduce | flops 192 | bytes 1536 | tf_op jit(solution)/shard_map/psum | solution.py:49
  467.6 68.1 %all-reduce = (f32[128]{0:T(128)S(1)}, f32[128]{0:T(128)S(1)}) all-reduce(f32[128]{0:T(128)S(1)} %get-tuple-element.16, f32[128]{0:T(128)S(1)} %get-tuple-element.17), channel_id=1, replica_groups=mesh['row'=8,'col'=32] {'col'}, use_global_device_ids=true, to_apply=%region_8.0 | all-reduce | flops 256 | bytes 2048 | tf_op jit(solution)/shard_map/psum | solution.py:38
  535.7 1.6 fusion.23
  (16 shorter events, 0.2 us)
Async XLA Ops:
  7.2 180.8 %all-gather.4.cloned.1.call-start = ((), (), s32[]{:S(2)}) async-start(), calls=%async_computation.2 | async-start | bytes 1622016 | tf_op jit(solution)/shard_map/all_gather | solution.py:23
  141.3 151.5 %all-gather.6.cloned.1.call-start = ((), (), s32[]{:S(2)}) async-start(), calls=%async_computation.3 | async-start | bytes 10616832 | tf_op jit(solution)/shard_map/all_gather | solution.py:24
  142.0 224.4 %all-gather.8.cloned.1.call-start = ((), (), s32[]{:S(2)}) async-start(), calls=%async_computation.4 | async-start | bytes 1769472 | tf_op jit(solution)/shard_map/all_gather | solution.py:43
  300.1 152.2 %reduce-scatter.4.cloned.1.call-start = ((), (), s32[]{:S(2)}) async-start(), calls=%async_computation.5 | async-start | bytes 3244032 | tf_op jit(solution)/shard_map/reduce_scatter | solution.py:29
  309.4 1.5 copy-start
  366.4 2.4 copy-start.1
  368.8 83.5 %copy-start.2 = (bf16[128,192]{0,1:T(8,128)(2,1)S(1)}, bf16[128,192]{0,1:T(8,128)(2,1)}, u32[]{:S(2)}) copy-start(bf16[128,192]{0,1:T(8,128)(2,1)} %param.5) | copy-start | bytes 147460
  368.8 83.5 %copy-start.3 = (f32[192]{0:T(256)S(1)}, f32[192]{0:T(256)}, u32[]{:S(2)}) copy-start(f32[192]{0:T(256)} %param.6) | copy-start | bytes 2308
Sparse Core Ops, SparseCore 0:
  141.4 46.5 all-gather.3
  189.8 102.9 all-gather.5
  300.2 58.0 all-gather.7
  362.1 90.1 reduce-scatter.3
where the time goes:
time: 544 us
  blocking collectives  266 us (49%)
  waiting for transfers between devices  232 us (43%)
  matrix products  17.1 us (3%)
  between operations  13.8 us (3%)
  other arithmetic  10.1 us (2%)
    all_gather x1, waiting for transfers between devices, body(): weight_full = lax.all_gather(up_weight, 'row', axis=0, tiled=True)  105 us
    reduce_scatter x1, waiting for transfers between devices, body(): lax.psum_scatter(lax.dot_general(weight_full, pre_grad, (((1,), (1,)), ((...  80.6 us
    psum x1, blocking collectives, body(): lax.psum((jnp.sum(grads, axis=1), jnp.sum(grads * normed, axis=1)), 'col')  68.1 us
    psum x1, blocking collectives, body(): squares = lax.psum(jnp.sum(centred * centred, axis=1), 'col')  65.6 us
    psum x1, blocking collectives, body(): total = lax.psum(jnp.sum(xf, axis=1), 'col')  65.3 us
    all_to_all x1, blocking collectives, body(): lax.all_to_all(scaled_full, 'row', split_axis=1, concat_axis=0, tiled=True)  53 us
    all_gather x1, waiting for transfers between devices, body(): scaled_full = lax.all_gather(scaled, 'col', axis=1, tiled=True)  45.9 us
    psum x1, blocking collectives, body(): gain_grad = lax.psum(gain_part, 'row')  14.3 us
  transfers between devices with their start and end apart: 4, of which 3 were waited for; matrix products, arithmetic and copies ran while one was open for 3% of the time, Pallas kernels for 0%

commit v1 on v0

v1 whole, which is shorter than its diff:
```python
import functools

import jax
import jax.numpy as jnp
from jax import lax
from jax.experimental import pallas as pl
from jax.experimental.pallas import tpu as pltpu
from jax.sharding import PartitionSpec as P

D = 6144
F = 192
T = 128
K = 768
HALF = K // 2
MESH = pl.DeviceIdType.MESH
F32 = jnp.float32
BF16 = jnp.bfloat16
SQRT_HALF = 0.7071067811865476
INV_SQRT_2PI = 0.3989422804014327


def split3(row):
    hi = row.astype(BF16).astype(F32)
    rest = row - hi
    mid = rest.astype(BF16).astype(F32)
    low = rest - mid
    at = lax.broadcasted_iota(jnp.int32, (8, row.shape[1]), 0)
    rows = jnp.where(at == 0, hi, jnp.where(at == 1, mid, jnp.where(at == 2, low, 0.0)))
    return rows.astype(BF16)


def dot_nt(a, b):
    return lax.dot_general(a, b, (((1,), (1,)), ((), ())), preferred_element_type=F32)


def kernel(
    tok_ref, gain_ref, w_ref, bias_ref, cot_ref,
    act_ref, xg_ref, wg_ref, bg_ref, gg_ref,
    chunk, normt, gaint, stat1, stat2, xb, part, pre, pg,
    rs_out, rs_in, ce_out, ce_in, rb_out, rb_in, own, ra_out, ra_in, home_out, home_in,
    wz, gz,
    s1_s, s1_r, s2_s, s2_r, sh_s, sh_r, xa_s, xa_r, xb_s, xb_r, xc_s, xc_r,
    wz_s, wz_r, gz_s, gz_r, rs_s, rs_r, ag_s, ag_r, ce_s, ce_r, rb_s, rb_r, ra_s, ra_r, hm_s, hm_r,
):
    r = lax.axis_index("row")
    c = lax.axis_index("col")
    y = c // 8
    x = (c // 2) % 4
    e = c % 2
    a = (1 - e) * x + e * y
    b = (1 - e) * y + e * x

    def at(z, yy, xx, ee):
        return (z, (yy * 4 + xx) * 2 + ee)

    def place(z, aa, bb, ee):
        return at(z, (1 - ee) * bb + ee * aa, (1 - ee) * aa + ee * bb, ee)

    def zpeer(j):
        return at((r + j) % 8, y, x, e)

    def apeer(j):
        return place(r, (a + j) % 4, b, e)

    def bpeer(j):
        return place(r, a, (b + j) % 4, e)

    core = at(r, y, x, 1 - e)
    my_k = (a + 3) % 4
    my_q = 2 * ((b + 3) % 4) + e
    owner = place(c // 4, (c % 4 + 1) % 4, (r // 2 + 1) % 4, r % 2)
    home = (my_q, 4 * r + my_k)

    peers = [zpeer(j) for j in range(1, 8)]
    peers += [apeer(j) for j in (1, 2, 3)] + [bpeer(j) for j in (1, 2, 3)]
    peers += [core, owner, home]
    barrier = pltpu.get_barrier_semaphore()
    for peer in peers:
        pl.semaphore_signal(barrier, inc=1, device_id=peer, device_id_type=MESH)
    pl.semaphore_wait(barrier, len(peers))

    def send(src, dst, ssem, rsem, to):
        return pltpu.make_async_remote_copy(
            src_ref=src, dst_ref=dst, send_sem=ssem, recv_sem=rsem, device_id=to, device_id_type=MESH
        )

    def arrived(dst, ssem, rsem):
        send(dst, dst, ssem, rsem, core).wait_recv()

    pending = []

    def go(src, dst, ssem, rsem, to):
        copy = send(src, dst, ssem, rsem, to)
        copy.start()
        pending.append(copy)

    def plane_gather(tiles, ssem, rsem):
        mine = (e * 4 + b) * 4
        for j in (1, 2, 3):
            ref = tiles.at[mine + a]
            go(ref, ref, ssem.at[j - 1], rsem.at[j - 1], apeer(j))
        yield
        for j in (1, 2, 3):
            arrived(tiles.at[mine + (a + 4 - j) % 4], ssem.at[j - 1], rsem.at[j - 1])
        for j in (1, 2, 3):
            ref = tiles.at[pl.ds(mine, 4)]
            go(ref, ref, ssem.at[j + 2], rsem.at[j + 2], bpeer(j))
        yield
        for j in (1, 2, 3):
            ref = tiles.at[pl.ds((e * 4 + (b + 4 - j) % 4) * 4, 4)]
            arrived(ref, ssem.at[j + 2], rsem.at[j + 2])
        ref = tiles.at[pl.ds(e * 16, 16)]
        go(ref, ref, ssem.at[6], rsem.at[6], core)
        yield
        arrived(tiles.at[pl.ds((1 - e) * 16, 16)], ssem.at[6], rsem.at[6])
        yield

    xt = tok_ref[...].astype(F32).T
    gaint[...] = jnp.broadcast_to(gain_ref[...], (T, F)).T
    total = jnp.sum(xt, axis=0, keepdims=True)
    dev = xt - total / F
    squares = jnp.sum(dev * dev, axis=0, keepdims=True)
    slot = (e * 4 + b) * 4 + a
    stat1[slot] = jnp.zeros((8, T), F32)
    stat1[slot, 0:1, :] = total
    stat1[slot, 1:2, :] = squares
    stat1[slot, 2:3, :] = gain_ref[:, 0:128]
    stat1[slot, 3:4, 0:64] = gain_ref[:, 128:192]
    for _ in plane_gather(stat1, s1_s, s1_r):
        pass
    sums = stat1[:, 0, :]
    mean = jnp.sum(sums, axis=0, keepdims=True) / D
    apart = sums / F - mean
    var = (
        jnp.sum(stat1[:, 1, :], axis=0, keepdims=True)
        + F * jnp.sum(apart * apart, axis=0, keepdims=True)
    ) / D
    rstd = lax.rsqrt(var + 1e-06)
    normed = (xt - mean) * rstd
    normt[...] = normed
    chunk[...] = (normed * gaint[...]).astype(BF16)

    mine = pl.ds(pl.multiple_of(my_k * F, F), F)
    go(chunk, xb.at[r, pl.ds(pl.multiple_of((c % 4) * F, F), F)], sh_s, sh_r, owner)

    wbar = jnp.zeros((8, K), F32)
    for k in range(4):
        col = 4 * r + k
        cy, cx, ce = col // 8, (col // 2) % 4, col % 2
        gslot = (ce * 4 + (1 - ce) * cy + ce * cx) * 4 + (1 - ce) * cx + ce * cy
        grow = jnp.concatenate([stat1[gslot, 2:3, :], stat1[gslot, 3:4, 0:64]], axis=1)
        wbar += jnp.dot(split3(grow), w_ref[k * F:(k + 1) * F, :], preferred_element_type=F32)
    wz[r] = jnp.sum(wbar, axis=0, keepdims=True)

    ref = xb.at[my_q, mine]
    arrived(ref, sh_s, sh_r)
    for j in (1, 2, 3):
        go(ref, ref, xa_s.at[j - 1], xa_r.at[j - 1], apeer(j))
    for j in range(1, 8):
        go(wz.at[r], wz.at[r], wz_s.at[j - 1], wz_r.at[j - 1], zpeer(j))
    for j in (1, 2, 3):
        k = (my_k + 4 - j) % 4
        arrived(xb.at[my_q, pl.ds(pl.multiple_of(k * F, F), F)], xa_s.at[j - 1], xa_r.at[j - 1])
    ref = xb.at[my_q]
    for j in (1, 2, 3):
        go(ref, ref, xb_s.at[j - 1], xb_r.at[j - 1], bpeer(j))
    go(ref, ref, xc_s.at[0], xc_r.at[0], core)
    for j in (1, 3, 2):
        q = 2 * ((b + 3 + 4 - j) % 4) + e
        ref = xb.at[q]
        arrived(ref, xb_s.at[j - 1], xb_r.at[j - 1])
        go(ref, ref, xc_s.at[j], xc_r.at[j], core)
    for j in (0, 1, 3, 2):
        q = 2 * ((a + 3 + 4 - j) % 4) + 1 - e
        arrived(xb.at[q], xc_s.at[j], xc_r.at[j])

    def product(i, carry):
        odd = i % 2
        q = (r + (1 - odd) * (4 + i // 2) + odd * (3 - i // 2)) % 8
        part[q] = jnp.dot(xb[q].T, w_ref[...], preferred_element_type=F32)
        return carry

    def rs_slot(way, half, s):
        return (way * 2 + half) * 4 + s

    def rs_step(s):
        for half_of_plus in (0, 1):
            for way in (0, 1):
                half = half_of_plus if way == 0 else 1 - half_of_plus
                first = 0 if half_of_plus == 0 else 1
                if s < first:
                    continue
                cols = slice(half * HALF, (half + 1) * HALF)
                q = (r + 4 - s) % 8 if way == 0 else (r + 4 + s) % 8
                value = part[q, :, cols]
                n = rs_slot(way, half, s)
                if s > first:
                    arrived(rs_in.at[n - 1], rs_s.at[n - 1], rs_r.at[n - 1])
                    value = value + rs_in[n - 1].astype(F32)
                rs_out[n] = value.astype(BF16)
                to = zpeer(1) if way == 0 else zpeer(7)
                go(rs_out.at[n], rs_in.at[n], rs_s.at[n], rs_r.at[n], to)

    lax.fori_loop(0, 1, product, 0)
    rs_step(0)
    lax.fori_loop(1, 3, product, 0)
    rs_step(1)
    lax.fori_loop(3, 8, product, 0)
    rs_step(2)
    rs_step(3)
    for j in range(1, 8):
        arrived(wz.at[(r + 8 - j) % 8], wz_s.at[j - 1], wz_r.at[j - 1])
    wsum = split3(jnp.sum(wz[...], axis=0))
    for way in (0, 1):
        for half in (0, 1):
            n = rs_slot(way, half, 3)
            arrived(rs_in.at[n], rs_s.at[n], rs_r.at[n])

    def gelu(i, carry):
        rows = pl.ds(pl.multiple_of(i * 16, 16), 16)
        both = []
        for half in (0, 1):
            cols = slice(half * HALF, (half + 1) * HALF)
            both.append(
                part[r, rows, cols]
                + rs_in[rs_slot(0, half, 3), rows, :].astype(F32)
                + rs_in[rs_slot(1, half, 3), rows, :].astype(F32)
            )
        raw = jnp.concatenate(both, axis=1)
        v = raw + bias_ref[...]
        phi = 0.5 * (1.0 + lax.erf(v * SQRT_HALF))
        act_ref[rows, :] = (v * phi).astype(BF16)
        slope = phi + v * (INV_SQRT_2PI * jnp.exp(-0.5 * v * v))
        grad = (cot_ref[rows, :].astype(F32) * slope).astype(BF16)
        pg[r, rows, :] = grad
        pre[rows, :] = jnp.broadcast_to(
            jnp.sum(grad.astype(F32) * raw, axis=1, keepdims=True), (16, T)
        )
        return carry

    lax.fori_loop(0, 8, gelu, 0)

    def ag_send(t):
        for half_of_plus in (0, 1):
            for way in (0, 1):
                half = half_of_plus if way == 0 else 1 - half_of_plus
                if t == 4 and half_of_plus == 1:
                    continue
                q = (r + 8 - (t - 1)) % 8 if way == 0 else (r + t - 1) % 8
                n = (way * 2 + half) * 4 + t - 1
                ref = pg.at[q, :, pl.ds(half * HALF, HALF)]
                if t > 1:
                    arrived(ref, ag_s.at[n - 1], ag_r.at[n - 1])
                to = zpeer(1) if way == 0 else zpeer(7)
                go(ref, ref, ag_s.at[n], ag_r.at[n], to)

    def ag_rest(last):
        for way in (0, 1):
            half = way if last == 4 else 1 - way
            n = (way * 2 + half) * 4 + last - 1
            q = (r + 8 - last) % 8 if way == 0 else (r + last) % 8
            ref = pg.at[q, :, pl.ds(half * HALF, HALF)]
            arrived(ref, ag_s.at[n], ag_r.at[n])

    def back(q):
        return dot_nt(w_ref[...], pg[q])

    swap = (r + e) % 2
    conditional = []

    def pair(p, even, odd):
        q_mine = (r + 8 + (1 - swap) * even + swap * odd) % 8
        q_other = (r + 8 + (1 - swap) * odd + swap * even) % 8
        ce_out[p] = back(q_other).astype(BF16)
        go(ce_out.at[p], ce_in.at[p], ce_s.at[p], ce_r.at[p], core)
        value = back(q_mine)
        arrived(ce_in.at[p], ce_s.at[p], ce_r.at[p])
        value = value + ce_in[p].astype(F32)
        b_to = (q_mine // 2 + 1) % 4

        @pl.when(b_to == b)
        def _():
            own[...] = value

        @pl.when(b_to != b)
        def _():
            rb_out[p] = value.astype(BF16)
            send(rb_out.at[p], rb_in.at[b], rb_s.at[p], rb_r.at[b], place(r, a, b_to, e)).start()

        conditional.append((p, b_to))

    ag_send(1)
    second_col = pre[...].T[0:1, :]
    first = jnp.sum(dot_nt(wsum, pg[r]), axis=0, keepdims=True)
    stat2[slot] = jnp.zeros((8, T), F32)
    stat2[slot, 0:1, :] = first
    stat2[slot, 1:2, :] = second_col
    gather = plane_gather(stat2, s2_s, s2_r)
    next(gather)
    ag_send(2)
    next(gather)
    pair(0, 0, 1)
    ag_send(3)
    next(gather)
    pair(1, 2, -1)
    ag_send(4)
    next(gather)
    ag_rest(3)
    pair(2, -2, 3)
    ag_rest(4)
    pair(3, 4, -3)

    def weight(i, carry):
        rows = pl.ds(pl.multiple_of(i * 128, 128), 128)
        lhs = jnp.concatenate([xb[q, rows, :] for q in range(8)], axis=1)
        wg_ref[rows, :] = jnp.dot(lhs, pg[...].reshape(8 * T, K), preferred_element_type=F32)
        return carry

    lax.fori_loop(0, 6, weight, 0)
    ones = jnp.ones((16, 8 * T), BF16)
    bg_ref[...] = jnp.dot(ones, pg[...].reshape(8 * T, K), preferred_element_type=F32)[0:1, :]

    for j in (1, 2, 3):
        n = (b + j) % 4
        arrived(rb_in.at[n], rb_s.at[0], rb_r.at[n])
        own[...] += rb_in[n].astype(F32)
    for j in (1, 2, 3):
        k = (my_k + j) % 4
        ra_out[j - 1] = own[pl.ds(pl.multiple_of(k * F, F), F), :].astype(BF16)
        go(ra_out.at[j - 1], ra_in.at[j - 1], ra_s.at[j - 1], ra_r.at[j - 1], apeer(j))
    value = own[mine, :]
    for j in (1, 2, 3):
        arrived(ra_in.at[j - 1], ra_s.at[j - 1], ra_r.at[j - 1])
        value = value + ra_in[j - 1].astype(F32)
    home_out[...] = value.astype(BF16)
    go(home_out, home_in, hm_s, hm_r, home)
    arrived(home_in, hm_s, hm_r)

    grad = home_in[...].astype(F32)
    normed = normt[...]
    gz[r] = jnp.sum((grad * normed).T, axis=0, keepdims=True)
    for j in range(1, 8):
        go(gz.at[r], gz.at[r], gz_s.at[j - 1], gz_r.at[j - 1], zpeer(j))
    g = grad * gaint[...]
    first = jnp.sum(stat2[:, 0, :], axis=0, keepdims=True) / D
    second = jnp.sum(stat2[:, 1, :], axis=0, keepdims=True) / D
    xg_ref[...] = (rstd * (g - first - normed * second)).T.astype(BF16)
    for j in range(1, 8):
        arrived(gz.at[(r + 8 - j) % 8], gz_s.at[j - 1], gz_r.at[j - 1])
    gg_ref[...] = jnp.sum(gz[...], axis=0)

    for copy in pending:
        copy.wait_send()
    for p, b_to in conditional:
        @pl.when(b_to != b)
        def _():
            send(rb_out.at[p], rb_in.at[b], rb_s.at[p], rb_r.at[b], core).wait_send()


def body(tokens, norm_gain, up_weight, up_bias, cotangent):
    def vmem(shape, dtype):
        return pltpu.VMEM(shape, dtype)

    def sems(*shape):
        return pltpu.SemaphoreType.DMA(shape)

    scratch = [
        vmem((F, T), BF16), vmem((F, T), F32), vmem((F, T), F32),
        vmem((32, 8, T), F32), vmem((32, 8, T), F32),
        vmem((8, K, T), BF16), vmem((8, T, K), F32), vmem((T, T), F32), vmem((8, T, K), BF16),
        vmem((16, T, HALF), BF16), vmem((16, T, HALF), BF16),
        vmem((4, K, T), BF16), vmem((4, K, T), BF16),
        vmem((4, K, T), BF16), vmem((4, K, T), BF16), vmem((K, T), F32),
        vmem((3, F, T), BF16), vmem((3, F, T), BF16), vmem((F, T), BF16), vmem((F, T), BF16),
        vmem((8, 1, K), F32), vmem((8, 1, F), F32),
    ]
    scratch += [
        sems(7), sems(7), sems(7), sems(7), sems(), sems(), sems(3), sems(3), sems(3), sems(3),
        sems(4), sems(4), sems(7), sems(7), sems(7), sems(7), sems(16), sems(16), sems(16), sems(16),
        sems(4), sems(4), sems(4), sems(4), sems(3), sems(3), sems(), sems(),
    ]
    space = pl.BlockSpec(memory_space=pltpu.VMEM)
    act, xg, wg, bg, gg = pl.pallas_call(
        kernel,
        out_shape=[
            jax.ShapeDtypeStruct((T, K), BF16),
            jax.ShapeDtypeStruct((T, F), BF16),
            jax.ShapeDtypeStruct((K, K), F32),
            jax.ShapeDtypeStruct((1, K), F32),
            jax.ShapeDtypeStruct((1, F), F32),
        ],
        in_specs=[space] * 5,
        out_specs=[space] * 5,
        scratch_shapes=scratch,
        compiler_params=pltpu.CompilerParams(
            collective_id=0, has_side_effects=True, vmem_limit_bytes=48 * 2**20
        ),
        name="mlp_up",
    )(tokens, norm_gain.reshape(1, F), up_weight, up_bias.reshape(1, K), cotangent)
    return act, xg, wg, bg.reshape(K), gg.reshape(F)


def solution(mesh):
    in_specs = (P("row", "col"), P("col"), P("row", "col"), P("col"), P("row", "col"))
    out_specs = (P("row", "col"), P("row", "col"), P("row", "col"), P("col"), P("col"))
    return jax.shard_map(body, mesh=mesh, in_specs=in_specs, out_specs=out_specs, check_vma=False)
```

time: 544 us -> 117 us (0.22)
  blocking collectives: 266 us -> 0 us
  waiting for transfers between devices: 232 us -> 0 us
  Pallas kernels: 0 us -> 108 us
  matrix products: 17.1 us -> 0 us
  between operations: 13.8 us -> 0.65 us
  other arithmetic: 10.1 us -> 0.6 us
    psum x4 -> x0, blocking collectives: 213 us -> none  [the longest x1 68.1 us: body(): lax.psum((jnp.sum(grads, axis=1), jnp.sum(grads * normed, axis=1)), 'col')]
    all_gather x3 -> x0, waiting for transfers between devices: 151 us -> none  [the longest x1 105 us: body(): weight_full = lax.all_gather(up_weight, 'row', axis=0, tiled=True)]
    pallas_call x0 -> x1, Pallas kernels: none -> 108 us  [body(): pl.pallas_call(kernel, out_shape=[jax.ShapeDtypeStruct((T, K), BF16), jax...]
    reduce_scatter x1 -> x0, waiting for transfers between devices: 80.6 us -> none  [body(): lax.psum_scatter(lax.dot_general(weight_full, pre_grad, (((1,), (1,)), ((...]
    all_to_all x1 -> x0, blocking collectives: 53 us -> none  [body(): lax.all_to_all(scaled_full, 'row', split_axis=1, concat_axis=0, tiled=True)]
    dot_general x3 -> x0, matrix products: 17.1 us -> none  [the longest x1 7.35 us: body(): jnp.dot(scaled_full, weight_full, preferred_element_type=jnp.float32)]
  transfers between devices with their start and end apart: 4 -> 0, of which waited for: 3 -> 0; matrix products, arithmetic and copies ran while one was open for 3% -> 0% of each run, Pallas kernels for 0% -> 0%
where the time goes in v1:
time: 117 us
  Pallas kernels  108 us (92%)
  local copies, waits for them, and re-layouts  7.83 us (7%)
    pallas_call x1, Pallas kernels, body(): pl.pallas_call(kernel, out_shape=[jax.ShapeDtypeStruct((T, K), BF16), jax...  108 us
    unnamed x11, local copies, waits for them, and re-layouts  7.14 us

profile of v1, /device:TPU:1, one launch (start us, length us, event | category | flops | bytes accessed | tf_op | source)
XLA Modules:
  0.0 116.8 jit_solution(10946758807845588398)
XLA Ops:
  0.6 0.9 copy.10.tok_ref
  1.5 0.7 reshape.23.bias_ref
  2.2 0.0 copy-start
  2.2 1.3 %copy-done = bf16[768,768]{1,0:T(8,128)(2,1)S(1)} copy-done((bf16[768,768]{1,0:T(8,128)(2,1)S(1)}, bf16[768,768]{1,0:T(8,128)(2,1)}, u32[]{:S(2)}) %copy-start) | copy-done | bytes 1179672
  3.5 0.0 copy-start.1
  3.5 0.9 copy-done.1
  4.4 0.0 copy-start.2
  4.4 0.7 copy-done.2
  5.1 107.7 %mlp_up.1 = (bf16[128,768]{1,0:T(8,128)(2,1)S(1)}, bf16[128,192]{1,0:T(8,128)(2,1)S(1)}, f32[768,768]{1,0:T(8,128)S(1)}, f32[1,768]{1,0:T(1,128)S(1)}, f32[1,192]{1,0:T(1,128)S(1)}) custom-call(bf16[128,192]{1,0:T(8,128)(2,1)S(1)} %copy.10.tok_ref, f32[1,192]{1,0:T(1,128)S(1)} %bitcast.3, bf16[768,768]{1,0:T(8,128)(2,1)S(1)} %copy-done, ...), custom_call_target="tpu_custom_call" | custom-call | tf_op jit(solution)/shard_map/mlp_up/pallas_call | solution.py:383
  112.8 0.7 copy.11
  113.5 0.6 reduce
  114.1 0.7 copy.15
  114.8 1.4 %copy.16 = f32[768,768]{1,0:T(8,128)} copy(f32[768,768]{1,0:T(8,128)S(1)} %get-tuple-element.27) | data formatting | bytes 4718592
  116.2 0.6 copy.17
Async XLA Ops:
  2.2 1.3 %copy-start = (bf16[768,768]{1,0:T(8,128)(2,1)S(1)}, bf16[768,768]{1,0:T(8,128)(2,1)}, u32[]{:S(2)}) copy-start(bf16[768,768]{1,0:T(8,128)(2,1)} %w_ref.1) | copy-start | bytes 3538948
  3.5 0.9 copy-start.1
  4.4 0.7 copy-start.2

commit v2 on v1

--- a/solution.py
+++ b/solution.py
@@ -34,14 +34,24 @@
 
 
 def kernel(
+    tok_hbm, gain_hbm, w_hbm, bias_hbm, cot_hbm,
+    act_ref, xg_ref, wg_ref, bg_ref, gg_ref,
     tok_ref, gain_ref, w_ref, bias_ref, cot_ref,
-    act_ref, xg_ref, wg_ref, bg_ref, gg_ref,
-    chunk, normt, gaint, stat1, stat2, xb, part, pre, pg,
+    normt, gaint, gaincol, stat1, stat2, zstat, xb, xn, part, pre, pg,
     rs_out, rs_in, ce_out, ce_in, rb_out, rb_in, own, ra_out, ra_in, home_out, home_in,
-    wz, gz,
-    s1_s, s1_r, s2_s, s2_r, sh_s, sh_r, xa_s, xa_r, xb_s, xb_r, xc_s, xc_r,
+    wz, gz_out, gz,
+    in_s, s1_s, s1_r, s2_s, s2_r, sh_s, sh_r, xa_s, xa_r, xb_s, xb_r, xc_s, xc_r, zs_s, zs_r,
     wz_s, wz_r, gz_s, gz_r, rs_s, rs_r, ag_s, ag_r, ce_s, ce_r, rb_s, rb_r, ra_s, ra_r, hm_s, hm_r,
 ):
+    loads = [
+        pltpu.make_async_copy(src, dst, in_s.at[i])
+        for i, (src, dst) in enumerate([
+            (tok_hbm, tok_ref), (gain_hbm, gain_ref), (w_hbm, w_ref), (bias_hbm, bias_ref), (cot_hbm, cot_ref),
+        ])
+    ]
+    for load in loads:
+        load.start()
+
     r = lax.axis_index("row")
     c = lax.axis_index("col")
     y = c // 8
@@ -68,16 +78,37 @@
     core = at(r, y, x, 1 - e)
     my_k = (a + 3) % 4
     my_q = 2 * ((b + 3) % 4) + e
+    mine = pl.ds(pl.multiple_of(my_k * F, F), F)
     owner = place(c // 4, (c % 4 + 1) % 4, (r // 2 + 1) % 4, r % 2)
     home = (my_q, 4 * r + my_k)
+
+    to_self = 4 * r + my_k == c
+
+    def holder(j):
+        return ((r + j) % 8, 4 * r + my_k)
+
+    def summer(q):
+        return place(c // 4, (c % 4 + 1) % 4, (q // 2 + 1) % 4, q % 2)
 
     peers = [zpeer(j) for j in range(1, 8)]
     peers += [apeer(j) for j in (1, 2, 3)] + [bpeer(j) for j in (1, 2, 3)]
     peers += [core, owner, home]
+    peers += [holder(j) for j in range(1, 8)]
+    sources = [q for q in range(8)]
     barrier = pltpu.get_barrier_semaphore()
     for peer in peers:
         pl.semaphore_signal(barrier, inc=1, device_id=peer, device_id_type=MESH)
-    pl.semaphore_wait(barrier, len(peers))
+
+    @pl.when(jnp.logical_not(to_self))
+    def _():
+        pl.semaphore_signal(barrier, inc=1, device_id=holder(0), device_id_type=MESH)
+
+    for q in sources:
+        @pl.when(jnp.logical_not(jnp.logical_and(to_self, my_q == q)))
+        def _():
+            pl.semaphore_signal(barrier, inc=1, device_id=summer(q), device_id_type=MESH)
+
+    pl.semaphore_wait(barrier, len(peers) + 9 - 2 * to_self.astype(jnp.int32))
 
     def send(src, dst, ssem, rsem, to):
         return pltpu.make_async_remote_copy(
@@ -115,8 +146,11 @@
         arrived(tiles.at[pl.ds((1 - e) * 16, 16)], ssem.at[6], rsem.at[6])
         yield
 
-    xt = tok_ref[...].astype(F32).T
-    gaint[...] = jnp.broadcast_to(gain_ref[...], (T, F)).T
+    loads[0].wait()
+    go(tok_ref, xb.at[r, pl.ds(pl.multiple_of((c % 4) * F, F), F)], sh_s, sh_r, owner)
+
+    loads[1].wait()
+    xt = tok_ref[...].astype(F32)
     total = jnp.sum(xt, axis=0, keepdims=True)
     dev = xt - total / F
     squares = jnp.sum(dev * dev, axis=0, keepdims=True)
@@ -126,8 +160,30 @@
     stat1[slot, 1:2, :] = squares
     stat1[slot, 2:3, :] = gain_ref[:, 0:128]
     stat1[slot, 3:4, 0:64] = gain_ref[:, 128:192]
-    for _ in plane_gather(stat1, s1_s, s1_r):
-        pass
+    gather = plane_gather(stat1, s1_s, s1_r)
+    next(gather)
+
+    def chunk(q, k):
+        return xb.at[q, pl.ds(pl.multiple_of(k * F, F), F)]
+
+    def spread(k, i):
+        for j in (1, 3, 2):
+            n = i * 3 + j - 1
+            go(chunk(my_q, k), chunk(my_q, k), xb_s.at[n], xb_r.at[n], bpeer(j))
+
+    ref = chunk(my_q, my_k)
+    arrived(ref, sh_s, sh_r)
+    for j in (1, 3, 2):
+        go(ref, ref, xa_s.at[j - 1], xa_r.at[j - 1], apeer(j))
+    spread(my_k, 0)
+    next(gather)
+    for j in (1, 3, 2):
+        k = (my_k + 4 - j) % 4
+        arrived(chunk(my_q, k), xa_s.at[j - 1], xa_r.at[j - 1])
+        spread(k, j)
+    go(xb.at[my_q], xb.at[my_q], xc_s.at[0], xc_r.at[0], core)
+    next(gather)
+    next(gather)
     sums = stat1[:, 0, :]
     mean = jnp.sum(sums, axis=0, keepdims=True) / D
     apart = sums / F - mean
@@ -136,48 +192,43 @@
         + F * jnp.sum(apart * apart, axis=0, keepdims=True)
     ) / D
     rstd = lax.rsqrt(var + 1e-06)
-    normed = (xt - mean) * rstd
-    normt[...] = normed
-    chunk[...] = (normed * gaint[...]).astype(BF16)
-
-    mine = pl.ds(pl.multiple_of(my_k * F, F), F)
-    go(chunk, xb.at[r, pl.ds(pl.multiple_of((c % 4) * F, F), F)], sh_s, sh_r, owner)
-
-    wbar = jnp.zeros((8, K), F32)
+    zstat[r] = jnp.zeros((8, T), F32)
+    zstat[r, 0:1, :] = mean
+    zstat[r, 1:2, :] = rstd
+    for j in range(1, 8):
+        go(zstat.at[r], zstat.at[r], zs_s.at[j - 1], zs_r.at[j - 1], zpeer(j))
+    gaint[...] = jnp.broadcast_to(gain_ref[...], (T, F)).T
+    normt[...] = (xt - mean) * rstd
+    grows = []
     for k in range(4):
         col = 4 * r + k
         cy, cx, ce = col // 8, (col // 2) % 4, col % 2
         gslot = (ce * 4 + (1 - ce) * cy + ce * cx) * 4 + (1 - ce) * cx + ce * cy
         grow = jnp.concatenate([stat1[gslot, 2:3, :], stat1[gslot, 3:4, 0:64]], axis=1)
-        wbar += jnp.dot(split3(grow), w_ref[k * F:(k + 1) * F, :], preferred_element_type=F32)
-    wz[r] = jnp.sum(wbar, axis=0, keepdims=True)
-
-    ref = xb.at[my_q, mine]
-    arrived(ref, sh_s, sh_r)
-    for j in (1, 2, 3):
-        go(ref, ref, xa_s.at[j - 1], xa_r.at[j - 1], apeer(j))
-    for j in range(1, 8):
-        go(wz.at[r], wz.at[r], wz_s.at[j - 1], wz_r.at[j - 1], zpeer(j))
-    for j in (1, 2, 3):
-        k = (my_k + 4 - j) % 4
-        arrived(xb.at[my_q, pl.ds(pl.multiple_of(k * F, F), F)], xa_s.at[j - 1], xa_r.at[j - 1])
-    ref = xb.at[my_q]
-    for j in (1, 2, 3):
-        go(ref, ref, xb_s.at[j - 1], xb_r.at[j - 1], bpeer(j))
-    go(ref, ref, xc_s.at[0], xc_r.at[0], core)
+        gaincol[k * F:(k + 1) * F, :] = jnp.broadcast_to(grow, (T, F)).T
+        grows.append(split3(grow))
     for j in (1, 3, 2):
         q = 2 * ((b + 3 + 4 - j) % 4) + e
-        ref = xb.at[q]
-        arrived(ref, xb_s.at[j - 1], xb_r.at[j - 1])
-        go(ref, ref, xc_s.at[j], xc_r.at[j], core)
+        for i in range(4):
+            k = (my_k + 4 - i) % 4
+            n = i * 3 + j - 1
+            arrived(chunk(q, k), xb_s.at[n], xb_r.at[n])
+        go(xb.at[q], xb.at[q], xc_s.at[j], xc_r.at[j], core)
+    for j in range(1, 8):
+        arrived(zstat.at[(r + 8 - j) % 8], zs_s.at[j - 1], zs_r.at[j - 1])
     for j in (0, 1, 3, 2):
         q = 2 * ((a + 3 + 4 - j) % 4) + 1 - e
         arrived(xb.at[q], xc_s.at[j], xc_r.at[j])
+    loads[2].wait()
 
     def product(i, carry):
         odd = i % 2
         q = (r + (1 - odd) * (4 + i // 2) + odd * (3 - i // 2)) % 8
-        part[q] = jnp.dot(xb[q].T, w_ref[...], preferred_element_type=F32)
+        for k in range(4):
+            rows = slice(k * F, (k + 1) * F)
+            normed = (xb[q, rows, :].astype(F32) - zstat[q, 0:1, :]) * zstat[q, 1:2, :]
+            xn[q, rows, :] = (normed * gaincol[rows, :]).astype(BF16)
+        part[q] = jnp.dot(xn[q].T, w_ref[...], preferred_element_type=F32)
         return carry
 
     def rs_slot(way, half, s):
@@ -207,14 +258,25 @@
     rs_step(1)
     lax.fori_loop(3, 8, product, 0)
     rs_step(2)
+    wbar = jnp.zeros((8, K), F32)
+    for k in range(4):
+        wbar += jnp.dot(grows[k], w_ref[k * F:(k + 1) * F, :], preferred_element_type=F32)
+    wz[r] = jnp.sum(wbar, axis=0, keepdims=True)
+    for j in range(1, 8):
+        go(wz.at[r], wz.at[r], wz_s.at[j - 1], wz_r.at[j - 1], zpeer(j))
     rs_step(3)
-    for j in range(1, 8):
-        arrived(wz.at[(r + 8 - j) % 8], wz_s.at[j - 1], wz_r.at[j - 1])
-    wsum = split3(jnp.sum(wz[...], axis=0))
+    loads[3].wait()
+    loads[4].wait()
     for way in (0, 1):
         for half in (0, 1):
             n = rs_slot(way, half, 3)
             arrived(rs_in.at[n], rs_s.at[n], rs_r.at[n])
+
+    for j in range(1, 8):
+        arrived(wz.at[(r + 8 - j) % 8], wz_s.at[j - 1], wz_r.at[j - 1])
+    wsum = split3(jnp.sum(wz[...], axis=0))
+
+    bias = bias_ref[...].reshape(1, K)
 
     def gelu(i, carry):
         rows = pl.ds(pl.multiple_of(i * 16, 16), 16)
@@ -227,7 +289,7 @@
                 + rs_in[rs_slot(1, half, 3), rows, :].astype(F32)
             )
         raw = jnp.concatenate(both, axis=1)
-        v = raw + bias_ref[...]
+        v = raw + bias
         phi = 0.5 * (1.0 + lax.erf(v * SQRT_HALF))
         act_ref[rows, :] = (v * phi).astype(BF16)
         slope = phi + v * (INV_SQRT_2PI * jnp.exp(-0.5 * v * v))
@@ -312,13 +374,13 @@
 
     def weight(i, carry):
         rows = pl.ds(pl.multiple_of(i * 128, 128), 128)
-        lhs = jnp.concatenate([xb[q, rows, :] for q in range(8)], axis=1)
+        lhs = jnp.concatenate([xn[q, rows, :] for q in range(8)], axis=1)
         wg_ref[rows, :] = jnp.dot(lhs, pg[...].reshape(8 * T, K), preferred_element_type=F32)
         return carry
 
     lax.fori_loop(0, 6, weight, 0)
     ones = jnp.ones((16, 8 * T), BF16)
-    bg_ref[...] = jnp.dot(ones, pg[...].reshape(8 * T, K), preferred_element_type=F32)[0:1, :]
+    bg_ref[...] = jnp.dot(ones, pg[...].reshape(8 * T, K), preferred_element_type=F32)[0:1, :].reshape(K)
 
     for j in (1, 2, 3):
         n = (b + j) % 4
@@ -332,22 +394,40 @@
     for j in (1, 2, 3):
         arrived(ra_in.at[j - 1], ra_s.at[j - 1], ra_r.at[j - 1])
         value = value + ra_in[j - 1].astype(F32)
-    home_out[...] = value.astype(BF16)
+    home_out[...] = value
     go(home_out, home_in, hm_s, hm_r, home)
-    arrived(home_in, hm_s, hm_r)
-
-    grad = home_in[...].astype(F32)
-    normed = normt[...]
-    gz[r] = jnp.sum((grad * normed).T, axis=0, keepdims=True)
+    normed = (xb[my_q, mine, :].astype(F32) - zstat[my_q, 0:1, :]) * zstat[my_q, 1:2, :]
+    row = jnp.sum((value * normed).T, axis=0, keepdims=True)
+    gz_out[...] = jnp.zeros((8, T), F32)
+    gz_out[0:1, :] = row[:, 0:128]
+    gz_out[1:2, 0:64] = row[:, 128:192]
     for j in range(1, 8):
-        go(gz.at[r], gz.at[r], gz_s.at[j - 1], gz_r.at[j - 1], zpeer(j))
-    g = grad * gaint[...]
+        go(gz_out, gz.at[my_q], gz_s.at[j], gz_r.at[my_q], holder(j))
+
+    @pl.when(to_self)
+    def _():
+        gz[my_q] = gz_out[...]
+
+    @pl.when(jnp.logical_not(to_self))
+    def _():
+        send(gz_out, gz.at[my_q], gz_s.at[0], gz_r.at[my_q], holder(0)).start()
+
     first = jnp.sum(stat2[:, 0, :], axis=0, keepdims=True) / D
     second = jnp.sum(stat2[:, 1, :], axis=0, keepdims=True) / D
-    xg_ref[...] = (rstd * (g - first - normed * second)).T.astype(BF16)
-    for j in range(1, 8):
-        arrived(gz.at[(r + 8 - j) % 8], gz_s.at[j - 1], gz_r.at[j - 1])
-    gg_ref[...] = jnp.sum(gz[...], axis=0)
+    arrived(home_in, hm_s, hm_r)
+    g = home_in[...] * gaint[...]
+    xg_ref[...] = (rstd * (g - first - normt[...] * second)).astype(BF16)
+    for q in sources:
+        @pl.when(jnp.logical_not(jnp.logical_and(to_self, my_q == q)))
+        def _():
+            arrived(gz.at[q], gz_s.at[0], gz_r.at[q])
+
+    row = jnp.sum(gz[...], axis=0)
+    gg_ref[...] = jnp.concatenate([row[0:1, :], row[1:2, 0:64]], axis=1)
+
+    @pl.when(jnp.logical_not(to_self))
+    def _():
+        send(gz_out, gz.at[my_q], gz_s.at[0], gz_r.at[my_q], holder(0)).wait_send()
 
     for copy in pending:
         copy.wait_send()
@@ -357,6 +437,15 @@
             send(rb_out.at[p], rb_in.at[b], rb_s.at[p], rb_r.at[b], core).wait_send()
 
 
+def store(*refs):
+    sem = refs[10]
+    copies = [pltpu.make_async_copy(refs[i], refs[5 + i], sem.at[i]) for i in range(5)]
+    for copy in copies:
+        copy.start()
+    for copy in copies:
+        copy.wait()
+
+
 def body(tokens, norm_gain, up_weight, up_bias, cotangent):
     def vmem(shape, dtype):
         return pltpu.VMEM(shape, dtype)
@@ -365,39 +454,50 @@
         return pltpu.SemaphoreType.DMA(shape)
 
     scratch = [
-        vmem((F, T), BF16), vmem((F, T), F32), vmem((F, T), F32),
-        vmem((32, 8, T), F32), vmem((32, 8, T), F32),
-        vmem((8, K, T), BF16), vmem((8, T, K), F32), vmem((T, T), F32), vmem((8, T, K), BF16),
+        vmem((F, T), BF16), vmem((1, F), F32), vmem((K, K), BF16), vmem((K,), F32), vmem((T, K), BF16),
+        vmem((F, T), F32), vmem((F, T), F32), vmem((K, T), F32),
+        vmem((32, 8, T), F32), vmem((32, 8, T), F32), vmem((8, 8, T), F32),
+        vmem((8, K, T), BF16), vmem((8, K, T), BF16), vmem((8, T, K), F32), vmem((T, T), F32), vmem((8, T, K), BF16),
         vmem((16, T, HALF), BF16), vmem((16, T, HALF), BF16),
         vmem((4, K, T), BF16), vmem((4, K, T), BF16),
         vmem((4, K, T), BF16), vmem((4, K, T), BF16), vmem((K, T), F32),
-        vmem((3, F, T), BF16), vmem((3, F, T), BF16), vmem((F, T), BF16), vmem((F, T), BF16),
-        vmem((8, 1, K), F32), vmem((8, 1, F), F32),
+        vmem((3, F, T), BF16), vmem((3, F, T), BF16), vmem((F, T), F32), vmem((F, T), F32),
+        vmem((8, 1, K), F32), vmem((8, T), F32), vmem((8, 8, T), F32),
     ]
     scratch += [
-        sems(7), sems(7), sems(7), sems(7), sems(), sems(), sems(3), sems(3), sems(3), sems(3),
-        sems(4), sems(4), sems(7), sems(7), sems(7), sems(7), sems(16), sems(16), sems(16), sems(16),
+        sems(5), sems(7), sems(7), sems(7), sems(7), sems(), sems(), sems(3), sems(3), sems(12), sems(12),
+        sems(4), sems(4), sems(7), sems(7), sems(7), sems(7), sems(8), sems(8), sems(16), sems(16), sems(16), sems(16),
         sems(4), sems(4), sems(4), sems(4), sems(3), sems(3), sems(), sems(),
     ]
     space = pl.BlockSpec(memory_space=pltpu.VMEM)
-    act, xg, wg, bg, gg = pl.pallas_call(
+    anywhere = pl.BlockSpec(memory_space=pl.ANY)
+    shapes = [
+        jax.ShapeDtypeStruct((T, K), BF16),
+        jax.ShapeDtypeStruct((F, T), BF16),
+        jax.ShapeDtypeStruct((K, K), F32),
+        jax.ShapeDtypeStruct((K,), F32),
+        jax.ShapeDtypeStruct((1, F), F32),
+    ]
+    results = pl.pallas_call(
         kernel,
-        out_shape=[
-            jax.ShapeDtypeStruct((T, K), BF16),
-            jax.ShapeDtypeStruct((T, F), BF16),
-            jax.ShapeDtypeStruct((K, K), F32),
-            jax.ShapeDtypeStruct((1, K), F32),
-            jax.ShapeDtypeStruct((1, F), F32),
-        ],
-        in_specs=[space] * 5,
+        out_shape=shapes,
+        in_specs=[pl.BlockSpec(memory_space=pltpu.HBM)] * 5,
         out_specs=[space] * 5,
         scratch_shapes=scratch,
         compiler_params=pltpu.CompilerParams(
             collective_id=0, has_side_effects=True, vmem_limit_bytes=48 * 2**20
         ),
         name="mlp_up",
-    )(tokens, norm_gain.reshape(1, F), up_weight, up_bias.reshape(1, K), cotangent)
-    return act, xg, wg, bg.reshape(K), gg.reshape(F)
+    )(tokens.T, norm_gain.reshape(1, F), up_weight, up_bias, cotangent)
+    act, xg, wg, bg, gg = pl.pallas_call(
+        store,
+        out_shape=shapes,
+        in_specs=[space] * 5,
+        out_specs=[anywhere] * 5,
+        scratch_shapes=[sems(5)],
+        name="store",
+    )(*results)
+    return act, xg.T, wg, bg, gg.reshape(F)
 
 
 def solution(mesh):

time: 117 us -> 107 us (0.915)
  Pallas kernels: 108 us -> 96.7 us
    pallas_call x1 -> x2, Pallas kernels: 108 us -> 96.7 us  [the longest x1 93.4 us: body(): pl.pallas_call(kernel, out_shape=shapes, in_specs=[pl.BlockSpec(memory_sp...]
    unnamed x11 -> x20, local copies, waits for them, and re-layouts: 7.14 us -> 8.2 us
where the time goes in v2:
time: 107 us; the launch traced here: 106 us
  Pallas kernels  96.7 us (90%)
  local copies, waits for them, and re-layouts  8.2 us (8%)
    pallas_call x1, Pallas kernels, body(): pl.pallas_call(kernel, out_shape=shapes, in_specs=[pl.BlockSpec(memory_sp...  93.4 us
    unnamed x20, local copies, waits for them, and re-layouts  8.2 us
    pallas_call x1, Pallas kernels, body(): pl.pallas_call(store, out_shape=shapes, in_specs=[space] * 5, out_specs=[...  3.35 us

profile of v2, /device:TPU:1, one launch (start us, length us, event | category | flops | bytes accessed | tf_op | source)
XLA Modules:
  0.0 105.6 jit_solution(13282970654656862211)
XLA Ops:
  0.6 0.0 copy-start.1
  0.6 1.3 %copy-done.1 = bf16[768,768]{1,0:T(8,128)(2,1)S(1)} copy-done((bf16[768,768]{1,0:T(8,128)(2,1)S(1)}, bf16[768,768]{1,0:T(8,128)(2,1)}, u32[]{:S(2)}) %copy-start.1) | copy-done | bytes 1179672
  1.9 0.0 copy-start.2
  1.9 0.9 copy-done.2
  2.8 0.0 copy-start.4
  2.8 0.8 copy-done.4
  3.6 0.0 copy-start.6
  3.6 0.7 copy-done.6
  4.3 0.0 copy-start.8
  4.3 0.7 copy-done.8
  5.0 93.4 %mlp_up.1 = (bf16[128,768]{1,0:T(8,128)(2,1)S(1)}, bf16[192,128]{1,0:T(8,128)(2,1)S(1)}, f32[768,768]{1,0:T(8,128)S(1)}, f32[768]{0:T(1024)S(1)}, f32[1,192]{1,0:T(1,128)S(1)}) custom-call(bf16[192,128]{1,0:T(8,128)(2,1)S(1)} %bitcast.4, f32[1,192]{1,0:T(1,128)S(1)} %bitcast.5, bf16[768,768]{1,0:T(8,128)(2,1)S(1)} %copy-done.1, f32[768]{0:T(1024)S(1)} %copy-done.6, ...), custom_call_target="tpu_custom_call" | custom-call | tf_op jit(solution)/shard_map/mlp_up/pallas_call | solution.py:481
  98.4 0.0 copy-start
  98.4 1.4 %copy-done = f32[768,768]{1,0:T(8,128)} copy-done((f32[768,768]{1,0:T(8,128)}, f32[768,768]{1,0:T(8,128)S(1)}, u32[]{:S(2)}) %copy-start) | copy-done | bytes 2359320
  99.8 0.0 copy-start.3
  99.8 0.7 copy-done.3
  100.5 0.0 copy-start.5
  100.5 0.6 copy-done.5
  101.1 0.0 copy-start.7
  101.1 0.6 copy-done.7
  101.7 0.0 copy-start.9
  101.7 0.6 copy-done.9
  102.2 3.3 %store.1 = (bf16[128,768]{1,0:T(8,128)(2,1)}, bf16[192,128]{1,0:T(8,128)(2,1)}, f32[768,768]{1,0:T(8,128)}, f32[768]{0:T(1024)}, f32[1,192]{1,0:T(1,128)}) custom-call(bf16[128,768]{1,0:T(8,128)(2,1)} %copy-done.3, bf16[192,128]{1,0:T(8,128)(2,1)} %copy-done.5, f32[768,768]{1,0:T(8,128)} %copy-done, f32[768]{0:T(1024)} %copy-done.7, f32[1,192]{1,0:T(1,128)} %copy-done.9), custom_call_target="tpu_custom_call" | custom-call | tf_op jit(solution)/shard_map/store/pallas_call | solution.py:492
Async XLA Ops:
  0.6 1.3 %copy-start.1 = (bf16[768,768]{1,0:T(8,128)(2,1)S(1)}, bf16[768,768]{1,0:T(8,128)(2,1)}, u32[]{:S(2)}) copy-start(bf16[768,768]{1,0:T(8,128)(2,1)} %w_hbm.1) | copy-start | bytes 3538948
  1.9 0.9 copy-start.2
  2.8 0.8 copy-start.4
  3.6 0.7 copy-start.6
  4.3 0.7 copy-start.8
  98.4 1.4 %copy-start = (f32[768,768]{1,0:T(8,128)}, f32[768,768]{1,0:T(8,128)S(1)}, u32[]{:S(2)}) copy-start(f32[768,768]{1,0:T(8,128)S(1)} %get-tuple-element.17.refs_2_) | copy-start | bytes 7077892
  99.8 0.7 copy-start.3
  100.5 0.6 copy-start.5
  101.1 0.6 copy-start.7
  101.7 0.6 copy-start.9

commit v3 on v2

v3 whole, which is shorter than its diff:
```python
import functools

import jax
import jax.numpy as jnp
from jax import lax
from jax.experimental import pallas as pl
from jax.experimental.pallas import tpu as pltpu
from jax.sharding import PartitionSpec as P

D = 6144
F = 192
S = F // 4
T = 128
K = 768
G = 4
ROWS = T // G
MESH = pl.DeviceIdType.MESH
F32 = jnp.float32
BF16 = jnp.bfloat16
SQRT_HALF = 0.7071067811865476
INV_SQRT_2PI = 0.3989422804014327


def split3(row):
    hi = row.astype(BF16).astype(F32)
    rest = row - hi
    mid = rest.astype(BF16).astype(F32)
    low = rest - mid
    at = lax.broadcasted_iota(jnp.int32, (8, row.shape[1]), 0)
    rows = jnp.where(at == 0, hi, jnp.where(at == 1, mid, jnp.where(at == 2, low, 0.0)))
    return rows.astype(BF16)


def dot_nt(a, b):
    return lax.dot_general(a, b, (((1,), (1,)), ((), ())), preferred_element_type=F32)


def kernel(
    tok_hbm, gain_hbm, w_hbm, bias_hbm, cot_hbm,
    act_hbm, xg_hbm, wg_hbm, bg_hbm, gg_hbm,
    tok_ref, gain_ref, w_ref, bias_ref, cot_ref,
    normt, gaint, gaincol, stat1, stat2, zstat, xb, xn, part, pre, pg,
    rs_out, rs_in, ce_out, ce_in, ra_out, ra_in, rb_out, rb_in, home_out, home_in, dots, own,
    wz, gz_out, gz, act_ref, xg_ref, wg_ref, bg_ref, gg_ref,
    in_s, out_s, s1_s, s1_r, s2_s, s2_r, sh_s, sh_r, xa_s, xa_r, xb_s, xb_r, xc_s, xc_r, zs_s, zs_r,
    wz_s, wz_r, gz_s, gz_r, rs_s, rs_r, ag_s, ag_r, ce_s, ce_r, ra_s, ra_r, rb_s, rb_r, hm_s, hm_r,
):
    loads = [
        pltpu.make_async_copy(src, dst, in_s.at[i])
        for i, (src, dst) in enumerate([
            (tok_hbm, tok_ref), (gain_hbm, gain_ref), (w_hbm, w_ref), (bias_hbm, bias_ref), (cot_hbm, cot_ref),
        ])
    ]
    for load in loads:
        load.start()

    r = lax.axis_index("row")
    c = lax.axis_index("col")
    y = c // 8
    x = (c // 2) % 4
    e = c % 2
    a = (1 - e) * x + e * y
    b = (1 - e) * y + e * x

    def at(z, yy, xx, ee):
        return (z, (yy * 4 + xx) * 2 + ee)

    def place(z, aa, bb, ee):
        return at(z, (1 - ee) * bb + ee * aa, (1 - ee) * aa + ee * bb, ee)

    def zpeer(j):
        return at((r + j) % 8, y, x, e)

    def apeer(j):
        return place(r, (a + j) % 4, b, e)

    def bpeer(j):
        return place(r, a, (b + j) % 4, e)

    core = at(r, y, x, 1 - e)
    def turn(z):
        return (z // 2) % 2 + 2 * (1 - z % 2)

    def gatherer(k, bb, ee):
        z = c // 4
        return place(z, (k + 4 - turn(z)) % 4, bb, ee)

    my_k = (a + turn(r)) % 4
    my_q = 2 * b + e
    mine = pl.ds(pl.multiple_of(my_k * F, F), F)

    def holder(q):
        return (q, 4 * r + my_k)

    peers = [zpeer(j) for j in range(1, 8)]
    peers += [apeer(j) for j in (1, 2, 3)] + [bpeer(j) for j in (1, 2, 3)] + [core]
    peers += [holder(q) for q in range(8)]
    peers += [gatherer(c % 4, bb, ee) for bb in range(4) for ee in range(2)]
    barrier = pltpu.get_barrier_semaphore()
    for peer in peers:
        pl.semaphore_signal(barrier, inc=1, device_id=peer, device_id_type=MESH)

    pl.semaphore_wait(barrier, len(peers))

    def send(src, dst, ssem, rsem, to):
        return pltpu.make_async_remote_copy(
            src_ref=src, dst_ref=dst, send_sem=ssem, recv_sem=rsem, device_id=to, device_id_type=MESH
        )

    def arrived(dst, ssem, rsem):
        send(dst, dst, ssem, rsem, core).wait_recv()

    pending = []

    def go(src, dst, ssem, rsem, to):
        copy = send(src, dst, ssem, rsem, to)
        copy.start()
        pending.append(copy)

    def plane_gather(tiles, ssem, rsem):
        mine = (e * 4 + b) * 4
        for j in (1, 2, 3):
            ref = tiles.at[mine + a]
            go(ref, ref, ssem.at[j - 1], rsem.at[j - 1], apeer(j))
        yield
        for j in (1, 2, 3):
            arrived(tiles.at[mine + (a + 4 - j) % 4], ssem.at[j - 1], rsem.at[j - 1])
        for j in (1, 2, 3):
            ref = tiles.at[pl.ds(mine, 4)]
            go(ref, ref, ssem.at[j + 2], rsem.at[j + 2], bpeer(j))
        yield
        for j in (1, 2, 3):
            ref = tiles.at[pl.ds((e * 4 + (b + 4 - j) % 4) * 4, 4)]
            arrived(ref, ssem.at[j + 2], rsem.at[j + 2])
        ref = tiles.at[pl.ds(e * 16, 16)]
        go(ref, ref, ssem.at[6], rsem.at[6], core)
        yield
        arrived(tiles.at[pl.ds((1 - e) * 16, 16)], ssem.at[6], rsem.at[6])
        yield

    loads[0].wait()
    owner = gatherer(c % 4, r // 2, r % 2)
    go(tok_ref, xb.at[r, pl.ds(pl.multiple_of((c % 4) * F, F), F)], sh_s, sh_r, owner)

    loads[1].wait()
    xt = tok_ref[...].astype(F32)
    total = jnp.sum(xt, axis=0, keepdims=True)
    dev = xt - total / F
    squares = jnp.sum(dev * dev, axis=0, keepdims=True)
    slot = (e * 4 + b) * 4 + a
    stat1[slot] = jnp.zeros((8, T), F32)
    stat1[slot, 0:1, :] = total
    stat1[slot, 1:2, :] = squares
    stat1[slot, 2:3, :] = gain_ref[:, 0:128]
    stat1[slot, 3:4, 0:64] = gain_ref[:, 128:192]
    gather = plane_gather(stat1, s1_s, s1_r)
    next(gather)

    def chunk(q, k):
        return xb.at[q, pl.ds(pl.multiple_of(k * F, F), F)]

    def spread(k, i):
        for j in (1, 3, 2):
            n = i * 3 + j - 1
            go(chunk(my_q, k), chunk(my_q, k), xb_s.at[n], xb_r.at[n], bpeer(j))

    ref = chunk(my_q, my_k)
    arrived(ref, sh_s, sh_r)
    for j in (1, 3, 2):
        go(ref, ref, xa_s.at[j - 1], xa_r.at[j - 1], apeer(j))
    spread(my_k, 0)
    next(gather)
    for j in (1, 3, 2):
        k = (my_k + 4 - j) % 4
        arrived(chunk(my_q, k), xa_s.at[j - 1], xa_r.at[j - 1])
        spread(k, j)
    go(xb.at[my_q], xb.at[my_q], xc_s.at[0], xc_r.at[0], core)
    next(gather)
    next(gather)
    sums = stat1[:, 0, :]
    mean = jnp.sum(sums, axis=0, keepdims=True) / D
    apart = sums / F - mean
    var = (
        jnp.sum(stat1[:, 1, :], axis=0, keepdims=True)
        + F * jnp.sum(apart * apart, axis=0, keepdims=True)
    ) / D
    rstd = lax.rsqrt(var + 1e-06)
    zstat[r] = jnp.zeros((8, T), F32)
    zstat[r, 0:1, :] = mean
    zstat[r, 1:2, :] = rstd
    for j in range(1, 8):
        go(zstat.at[r], zstat.at[r], zs_s.at[j - 1], zs_r.at[j - 1], zpeer(j))
    for j in (1, 3, 2):
        q = 2 * ((b + 4 - j) % 4) + e
        for i in range(4):
            n = i * 3 + j - 1
            arrived(chunk(q, (my_k + 4 - i) % 4), xb_s.at[n], xb_r.at[n])
        go(xb.at[q], xb.at[q], xc_s.at[j], xc_r.at[j], core)
    grows = []
    for k in range(4):
        col = 4 * r + k
        cy, cx, ce = col // 8, (col // 2) % 4, col % 2
        gslot = (ce * 4 + (1 - ce) * cy + ce * cx) * 4 + (1 - ce) * cx + ce * cy
        grow = jnp.concatenate([stat1[gslot, 2:3, :], stat1[gslot, 3:4, 0:64]], axis=1)
        gaincol[k * F:(k + 1) * F, :] = jnp.broadcast_to(grow, (T, F)).T
        grows.append(split3(grow))
    loads[2].wait()
    for j in range(1, 8):
        arrived(zstat.at[(r + 8 - j) % 8], zs_s.at[j - 1], zs_r.at[j - 1])
    for j in (0, 1, 3, 2):
        q = 2 * ((a + 4 - j) % 4) + 1 - e
        arrived(xb.at[q], xc_s.at[j], xc_r.at[j])

    def product(i, carry):
        odd = i % 2
        q = (r + (1 - odd) * (4 + i // 2) + odd * (3 - i // 2)) % 8
        for k in range(4):
            rows = slice(k * F, (k + 1) * F)
            normed = (xb[q, rows, :].astype(F32) - zstat[q, 0:1, :]) * zstat[q, 1:2, :]
            xn[q, rows, :] = (normed * gaincol[rows, :]).astype(BF16)
        part[q] = jnp.dot(xn[q].T, w_ref[...], preferred_element_type=F32)
        return carry

    def slot_of(way, s, g):
        return (way * 4 + s) * G + g

    def rows_of(g):
        return pl.ds(g * ROWS, ROWS)

    def ahead(way):
        return zpeer(1) if way == 0 else zpeer(7)

    def rs_step(s, g, ways):
        for way in ways:
            first = 0 if way == g % 2 else 1
            if s < first:
                continue
            q = (r + 4 - s) % 8 if way == 0 else (r + 4 + s) % 8
            value = part[q, rows_of(g), :]
            n = slot_of(way, s, g)
            if s > first:
                m = slot_of(way, s - 1, g)
                arrived(rs_in.at[m], rs_s.at[m], rs_r.at[m])
                value = value + rs_in[m].astype(F32)
            rs_out[n] = value.astype(BF16)
            go(rs_out.at[n], rs_in.at[n], rs_s.at[n], rs_r.at[n], ahead(way))

    def ag_step(t, g):
        for way in (g % 2, 1 - g % 2):
            if t == 4 and way != g % 2:
                continue
            q = (r + 9 - t) % 8 if way == 0 else (r + t - 1) % 8
            ref = pg.at[q, rows_of(g)]
            n = slot_of(way, t - 1, g)
            if t > 1:
                m = slot_of(way, t - 2, g)
                arrived(ref, ag_s.at[m], ag_r.at[m])
            go(ref, ref, ag_s.at[n], ag_r.at[n], ahead(way))

    def ag_last(t, g):
        way = g % 2 if t == 4 else 1 - g % 2
        q = (r + 8 - t) % 8 if way == 0 else (r + t) % 8
        m = slot_of(way, t - 1, g)
        arrived(pg.at[q, rows_of(g)], ag_s.at[m], ag_r.at[m])

    lax.fori_loop(0, 1, product, 0)
    for g in range(G):
        rs_step(0, g, (g % 2,))
    lax.fori_loop(1, 3, product, 0)
    for g in range(G):
        rs_step(1, g, (1 - g % 2,))
    lax.fori_loop(3, 8, product, 0)
    for g in range(G):
        rs_step(1, g, (g % 2,))
    gaint[...] = jnp.broadcast_to(gain_ref[...], (T, F)).T
    normt[...] = (xt - mean) * rstd
    wbar = jnp.zeros((8, K), F32)
    for k in range(4):
        wbar += jnp.dot(grows[k], w_ref[k * F:(k + 1) * F, :], preferred_element_type=F32)
    wz[r] = jnp.sum(wbar, axis=0, keepdims=True)
    for j in range(1, 8):
        go(wz.at[r], wz.at[r], wz_s.at[j - 1], wz_r.at[j - 1], zpeer(j))
    for s in (2, 3):
        for g in range(G):
            rs_step(s, g, (g % 2, 1 - g % 2))
    loads[3].wait()
    loads[4].wait()
    bias = bias_ref[...].reshape(1, K)

    for g in range(G):
        rows = rows_of(g)
        raw = part[r, rows, :]
        for way in (g % 2, 1 - g % 2):
            m = slot_of(way, 3, g)
            arrived(rs_in.at[m], rs_s.at[m], rs_r.at[m])
            raw = raw + rs_in[m].astype(F32)
        v = raw + bias
        phi = 0.5 * (1.0 + lax.erf(v * SQRT_HALF))
        act_ref[rows, :] = (v * phi).astype(BF16)
        slope = phi + v * (INV_SQRT_2PI * jnp.exp(-0.5 * v * v))
        grad = (cot_ref[rows, :].astype(F32) * slope).astype(BF16)
        pg[r, rows, :] = grad
        ag_step(1, g)
        pre[rows, :] = jnp.broadcast_to(
            jnp.sum(grad.astype(F32) * raw, axis=1, keepdims=True), (ROWS, T)
        )
    stores = [
        pltpu.make_async_copy(src, dst, out_s.at[i])
        for i, (src, dst) in enumerate([
            (act_ref, act_hbm), (xg_ref, xg_hbm),
            (wg_ref.at[0:256], wg_hbm.at[0:256]), (wg_ref.at[256:512], wg_hbm.at[256:512]),
            (wg_ref.at[512:768], wg_hbm.at[512:768]), (bg_ref, bg_hbm), (gg_ref, gg_hbm),
        ])
    ]
    stores[0].start()
    for j in range(1, 8):
        arrived(wz.at[(r + 8 - j) % 8], wz_s.at[j - 1], wz_r.at[j - 1])
    wsum = split3(jnp.sum(wz[...], axis=0))

    swap = (r + e) % 2
    dots[...] = jnp.zeros((2 * T, T), F32)

    def pair(p, even, odd):
        q = (r + 8 + (1 - swap) * even + swap * odd) % 8
        q_other = (r + 8 + (1 - swap) * odd + swap * even) % 8
        both = dot_nt(w_ref[...], jnp.concatenate([pg[q_other], pg[q]], axis=0))
        ce_out[p] = both[:, :T].astype(BF16)
        go(ce_out.at[p], ce_in.at[p], ce_s.at[p], ce_r.at[p], core)
        own[p] = both[:, T:]
        yield
        arrived(ce_in.at[p], ce_s.at[p], ce_r.at[p])
        for j in (2, 1, 3):
            k = (my_k + j) % 4
            rows = pl.ds(pl.multiple_of(k * F, F), F)
            n = p * 3 + j - 1
            ra_out[n] = (own[p, rows, :] + ce_in[p, rows, :].astype(F32)).astype(BF16)
            go(ra_out.at[n], ra_in.at[n], ra_s.at[n], ra_r.at[n], apeer(j))
        value = own[p, mine, :] + ce_in[p, mine, :].astype(F32)
        yield
        for j in (1, 3, 2):
            n = p * 3 + j - 1
            arrived(ra_in.at[n], ra_s.at[n], ra_r.at[n])
            value = value + ra_in[n].astype(F32)
        own[p, 0:F, :] = value
        for j in (2, 1, 3):
            bb = (b + j) % 4
            n = p * 3 + j - 1
            rb_out[n] = own[p, pl.ds(pl.multiple_of(bb * S, S), S), :].astype(BF16)
            go(rb_out.at[n], rb_in.at[n], rb_s.at[n], rb_r.at[n], bpeer(j))
        yield
        at_b = pl.ds(pl.multiple_of(b * S, S), S)
        value = own[p, at_b, :]
        for j in (1, 3, 2):
            n = p * 3 + j - 1
            arrived(rb_in.at[n], rb_s.at[n], rb_r.at[n])
            value = value + rb_in[n].astype(F32)
        home_out[p] = value
        go(home_out.at[p], home_in.at[at_b], hm_s.at[p], hm_r.at[b], holder(q))
        raw = xb[q, pl.ds(pl.multiple_of(my_k * F + b * S, S), S), :].astype(F32)
        dots[at_b, :] += value * ((raw - zstat[q, 0:1, :]) * zstat[q, 1:2, :])
        yield

    def ag_all(t):
        for g in range(G):
            ag_step(t, g)

    second_col = pre[...].T[0:1, :]
    first = jnp.sum(dot_nt(wsum, pg[r]), axis=0, keepdims=True)
    stat2[slot] = jnp.zeros((8, T), F32)
    stat2[slot, 0:1, :] = first
    stat2[slot, 1:2, :] = second_col
    gather = plane_gather(stat2, s2_s, s2_r)
    next(gather)
    ag_all(2)
    next(gather)
    pairs = [pair(0, 0, 1), pair(1, 2, -1), pair(2, -2, 3), pair(3, 4, -3)]
    next(pairs[0])
    ag_all(3)
    next(gather)
    next(pairs[0])
    next(pairs[1])
    ag_all(4)
    next(gather)
    next(pairs[0])
    next(pairs[1])
    for g in range(G):
        ag_last(3, g)
    next(pairs[2])
    next(pairs[0])
    next(pairs[1])
    for g in range(G):
        ag_last(4, g)
    next(pairs[3])
    next(pairs[2])
    next(pairs[3])

    def weight(i):
        rows = slice(i * 256, (i + 1) * 256)
        lhs = jnp.concatenate([xn[q, rows, :] for q in range(8)], axis=1)
        wg_ref[rows, :] = jnp.dot(lhs, pg[...].reshape(8 * T, K), preferred_element_type=F32)
        stores[2 + i].start()

    weight(0)
    next(pairs[1])
    weight(1)
    next(pairs[2])
    next(pairs[3])
    weight(2)
    ones = jnp.ones((16, 8 * T), BF16)
    bg_ref[...] = jnp.dot(ones, pg[...].reshape(8 * T, K), preferred_element_type=F32)[0:1, :].reshape(K)
    stores[5].start()
    next(pairs[2])
    next(pairs[3])

    for half in (0, 1):
        gz_out[half:half + 1, :] = jnp.sum(dots[half * T:(half + 1) * T, :].T, axis=0, keepdims=True)
    gz_out[2:8, :] = jnp.zeros((6, T), F32)
    for q in range(8):
        go(gz_out, gz.at[e * 4 + b], gz_s.at[q], gz_r.at[e * 4 + b], holder(q))

    first = jnp.sum(stat2[:, 0, :], axis=0, keepdims=True) / D
    second = jnp.sum(stat2[:, 1, :], axis=0, keepdims=True) / D
    for n in range(4):
        arrived(home_in.at[n * S:(n + 1) * S], hm_s.at[0], hm_r.at[n])
    g = home_in[...] * gaint[...]
    xg_ref[...] = (rstd * (g - first - normt[...] * second)).astype(BF16)
    stores[1].start()
    for n in range(8):
        arrived(gz.at[n], gz_s.at[0], gz_r.at[n])
    row = jnp.sum(gz[...], axis=0)
    gg_ref[...] = jnp.concatenate([row[0:1, :], row[1:2, 0:64]], axis=1)
    stores[6].start()

    for copy in stores:
        copy.wait()
    for copy in pending:
        copy.wait_send()

def store(*refs):
    ins, outs, held = refs[:5], refs[5:10], refs[10:15]
    in_sem, out_sem = refs[15:]
    rows = K // 8
    parts = [(ins[i], held[i], outs[i]) for i in (0, 1, 3, 4)]
    for i in range(8):
        at = pl.ds(i * rows, rows)
        parts.append((ins[2].at[at], held[2].at[at], outs[2].at[at]))
    loads = [pltpu.make_async_copy(src, mid, in_sem.at[i]) for i, (src, mid, _) in enumerate(parts)]
    stores = [pltpu.make_async_copy(mid, dst, out_sem.at[i]) for i, (_, mid, dst) in enumerate(parts)]
    for load in loads:
        load.start()
    for load, copy in zip(loads, stores):
        load.wait()
        copy.start()
    for copy in stores:
        copy.wait()


def body(tokens, norm_gain, up_weight, up_bias, cotangent):
    def vmem(shape, dtype):
        return pltpu.VMEM(shape, dtype)

    def sems(*shape):
        return pltpu.SemaphoreType.DMA(shape)

    scratch = [
        vmem((F, T), BF16), vmem((1, F), F32), vmem((K, K), BF16), vmem((K,), F32), vmem((T, K), BF16),
        vmem((F, T), F32), vmem((F, T), F32), vmem((K, T), F32),
        vmem((32, 8, T), F32), vmem((32, 8, T), F32), vmem((8, 8, T), F32),
        vmem((8, K, T), BF16), vmem((8, K, T), BF16), vmem((8, T, K), F32), vmem((T, T), F32), vmem((8, T, K), BF16),
        vmem((8 * G, ROWS, K), BF16), vmem((8 * G, ROWS, K), BF16),
        vmem((4, K, T), BF16), vmem((4, K, T), BF16),
        vmem((12, F, T), BF16), vmem((12, F, T), BF16), vmem((12, S, T), BF16), vmem((12, S, T), BF16),
        vmem((4, S, T), F32), vmem((F, T), F32), vmem((2 * T, T), F32), vmem((4, K, T), F32),
        vmem((8, 1, K), F32), vmem((8, T), F32), vmem((8, 8, T), F32),
        vmem((T, K), BF16), vmem((F, T), BF16), vmem((K, K), F32), vmem((K,), F32), vmem((1, F), F32),
    ]
    scratch += [
        sems(5), sems(7), sems(7), sems(7), sems(7), sems(7), sems(), sems(), sems(3), sems(3), sems(12), sems(12),
        sems(4), sems(4), sems(7), sems(7), sems(7), sems(7), sems(8), sems(8),
        sems(8 * G), sems(8 * G), sems(8 * G), sems(8 * G),
        sems(4), sems(4), sems(12), sems(12), sems(12), sems(12), sems(4), sems(4),
    ]
    anywhere = pl.BlockSpec(memory_space=pl.ANY)
    shapes = [
        jax.ShapeDtypeStruct((T, K), BF16),
        jax.ShapeDtypeStruct((F, T), BF16),
        jax.ShapeDtypeStruct((K, K), F32),
        jax.ShapeDtypeStruct((K,), F32),
        jax.ShapeDtypeStruct((1, F), F32),
    ]
    results = pl.pallas_call(
        kernel,
        out_shape=shapes,
        in_specs=[pl.BlockSpec(memory_space=pltpu.HBM)] * 5,
        out_specs=[anywhere] * 5,
        scratch_shapes=scratch,
        compiler_params=pltpu.CompilerParams(
            collective_id=0, has_side_effects=True, vmem_limit_bytes=58 * 2**20
        ),
        name="mlp_up",
    )(tokens.T, norm_gain.reshape(1, F), up_weight, up_bias, cotangent)
    act, xg, wg, bg, gg = pl.pallas_call(
        store,
        out_shape=shapes,
        in_specs=[anywhere] * 5,
        out_specs=[anywhere] * 5,
        scratch_shapes=[vmem(t.shape, t.dtype) for t in shapes] + [sems(12), sems(12)],
        compiler_params=pltpu.CompilerParams(vmem_limit_bytes=60 * 2**20),
        name="store",
    )(*results)
    return act, xg.T, wg, bg, gg.reshape(F)


def solution(mesh):
    in_specs = (P("row", "col"), P("col"), P("row", "col"), P("col"), P("row", "col"))
    out_specs = (P("row", "col"), P("row", "col"), P("row", "col"), P("col"), P("col"))
    return jax.shard_map(body, mesh=mesh, in_specs=in_specs, out_specs=out_specs, check_vma=False)
```

time: 107 us -> 89.9 us (0.84)
  Pallas kernels: 96.7 us -> 88.4 us
  local copies, waits for them, and re-layouts: 8.2 us -> 0 us
    unnamed x20 -> x0, local copies, waits for them, and re-layouts: 8.2 us -> none
    pallas_call x1, Pallas kernels: 93.4 us -> 85.7 us  [body(): pl.pallas_call(kernel, out_shape=shapes, in_specs=[pl.BlockSpec(memory_sp...]
where the time goes in v3:
time: 89.9 us; the launch traced here: 89.1 us
  Pallas kernels  88.4 us (98%)
    pallas_call x1, Pallas kernels, body(): pl.pallas_call(kernel, out_shape=shapes, in_specs=[pl.BlockSpec(memory_sp...  85.7 us
    pallas_call x1, Pallas kernels, body(): pl.pallas_call(store, out_shape=shapes, in_specs=[anywhere] * 5, out_spec...  2.71 us

profile of v3, /device:TPU:1, one launch (start us, length us, event | category | flops | bytes accessed | tf_op | source)
XLA Modules:
  0.0 89.1 jit_solution(9510127466212462038)
XLA Ops:
  0.6 85.7 %mlp_up.1 = (bf16[128,768]{1,0:T(8,128)(2,1)}, bf16[192,128]{1,0:T(8,128)(2,1)}, f32[768,768]{1,0:T(8,128)}, f32[768]{0:T(1024)}, f32[1,192]{1,0:T(1,128)}) custom-call(bf16[192,128]{1,0:T(8,128)(2,1)} %bitcast.4, f32[1,192]{1,0:T(1,128)} %bitcast.5, bf16[768,768]{1,0:T(8,128)(2,1)} %w_hbm.1, f32[768]{0:T(1024)} %bias_hbm.1, bf16[128,768]{1,0:T(8,128)(2,1)} %cot_hbm.1), custom_call_target="tpu_custom_call" | custom-call | tf_op jit(solution)/shard_map/mlp_up/pallas_call | solution.py:491
  86.4 2.7 %store.1 = (bf16[128,768]{1,0:T(8,128)(2,1)}, bf16[192,128]{1,0:T(8,128)(2,1)}, f32[768,768]{1,0:T(8,128)}, f32[768]{0:T(1024)}, f32[1,192]{1,0:T(1,128)}) custom-call(bf16[128,768]{1,0:T(8,128)(2,1)} %get-tuple-element.15.refs_0_, bf16[192,128]{1,0:T(8,128)(2,1)} %get-tuple-element.16.refs_1_, f32[768,768]{1,0:T(8,128)} %get-tuple-element.17.refs_2_, ...), custom_call_target="tpu_custom_call" | custom-call | tf_op jit(solution)/shard_map/store/pallas_call | solution.py:502

commit v4 on v3

--- a/solution.py
+++ b/solution.py
@@ -9,7 +9,6 @@
 
 D = 6144
 F = 192
-S = F // 4
 T = 128
 K = 768
 G = 4
@@ -40,10 +39,10 @@
     act_hbm, xg_hbm, wg_hbm, bg_hbm, gg_hbm,
     tok_ref, gain_ref, w_ref, bias_ref, cot_ref,
     normt, gaint, gaincol, stat1, stat2, zstat, xb, xn, part, pre, pg,
-    rs_out, rs_in, ce_out, ce_in, ra_out, ra_in, rb_out, rb_in, home_out, home_in, dots, own,
+    rs_out, rs_in, ce_out, ce_in, ra_out, ra_in, home_out, home_in, dots, own,
     wz, gz_out, gz, act_ref, xg_ref, wg_ref, bg_ref, gg_ref,
     in_s, out_s, s1_s, s1_r, s2_s, s2_r, sh_s, sh_r, xa_s, xa_r, xb_s, xb_r, xc_s, xc_r, zs_s, zs_r,
-    wz_s, wz_r, gz_s, gz_r, rs_s, rs_r, ag_s, ag_r, ce_s, ce_r, ra_s, ra_r, rb_s, rb_r, hm_s, hm_r,
+    wz_s, wz_r, gz_s, gz_r, rs_s, rs_r, ag_s, ag_r, ce_s, ce_r, ra_s, ra_r, hm_s, hm_r,
 ):
     loads = [
         pltpu.make_async_copy(src, dst, in_s.at[i])
@@ -160,21 +159,16 @@
         return xb.at[q, pl.ds(pl.multiple_of(k * F, F), F)]
 
     def spread(k, i):
-        for j in (1, 3, 2):
+        for j in (2, 1, 3):
             n = i * 3 + j - 1
             go(chunk(my_q, k), chunk(my_q, k), xb_s.at[n], xb_r.at[n], bpeer(j))
 
+    next(gather)
     ref = chunk(my_q, my_k)
     arrived(ref, sh_s, sh_r)
-    for j in (1, 3, 2):
+    for j in (2, 1, 3):
         go(ref, ref, xa_s.at[j - 1], xa_r.at[j - 1], apeer(j))
     spread(my_k, 0)
-    next(gather)
-    for j in (1, 3, 2):
-        k = (my_k + 4 - j) % 4
-        arrived(chunk(my_q, k), xa_s.at[j - 1], xa_r.at[j - 1])
-        spread(k, j)
-    go(xb.at[my_q], xb.at[my_q], xc_s.at[0], xc_r.at[0], core)
     next(gather)
     next(gather)
     sums = stat1[:, 0, :]
@@ -190,6 +184,11 @@
     zstat[r, 1:2, :] = rstd
     for j in range(1, 8):
         go(zstat.at[r], zstat.at[r], zs_s.at[j - 1], zs_r.at[j - 1], zpeer(j))
+    for j in (1, 3, 2):
+        k = (my_k + 4 - j) % 4
+        arrived(chunk(my_q, k), xa_s.at[j - 1], xa_r.at[j - 1])
+        spread(k, j)
+    go(xb.at[my_q], xb.at[my_q], xc_s.at[0], xc_r.at[0], core)
     for j in (1, 3, 2):
         q = 2 * ((b + 4 - j) % 4) + e
         for i in range(4):
@@ -318,7 +317,7 @@
     wsum = split3(jnp.sum(wz[...], axis=0))
 
     swap = (r + e) % 2
-    dots[...] = jnp.zeros((2 * T, T), F32)
+    dots[...] = jnp.zeros((F, T), F32)
 
     def pair(p, even, odd):
         q = (r + 8 + (1 - swap) * even + swap * odd) % 8
@@ -341,23 +340,10 @@
             n = p * 3 + j - 1
             arrived(ra_in.at[n], ra_s.at[n], ra_r.at[n])
             value = value + ra_in[n].astype(F32)
-        own[p, 0:F, :] = value
-        for j in (2, 1, 3):
-            bb = (b + j) % 4
-            n = p * 3 + j - 1
-            rb_out[n] = own[p, pl.ds(pl.multiple_of(bb * S, S), S), :].astype(BF16)
-            go(rb_out.at[n], rb_in.at[n], rb_s.at[n], rb_r.at[n], bpeer(j))
-        yield
-        at_b = pl.ds(pl.multiple_of(b * S, S), S)
-        value = own[p, at_b, :]
-        for j in (1, 3, 2):
-            n = p * 3 + j - 1
-            arrived(rb_in.at[n], rb_s.at[n], rb_r.at[n])
-            value = value + rb_in[n].astype(F32)
-        home_out[p] = value
-        go(home_out.at[p], home_in.at[at_b], hm_s.at[p], hm_r.at[b], holder(q))
-        raw = xb[q, pl.ds(pl.multiple_of(my_k * F + b * S, S), S), :].astype(F32)
-        dots[at_b, :] += value * ((raw - zstat[q, 0:1, :]) * zstat[q, 1:2, :])
+        home_out[p] = value.astype(BF16)
+        go(home_out.at[p], home_in.at[b], hm_s.at[p], hm_r.at[b], holder(q))
+        raw = xb[q, mine, :].astype(F32)
+        dots[...] += value * ((raw - zstat[q, 0:1, :]) * zstat[q, 1:2, :])
         yield
 
     def ag_all(t):
@@ -386,7 +372,6 @@
     for g in range(G):
         ag_last(3, g)
     next(pairs[2])
-    next(pairs[0])
     next(pairs[1])
     for g in range(G):
         ag_last(4, g)
@@ -401,28 +386,28 @@
         stores[2 + i].start()
 
     weight(0)
-    next(pairs[1])
-    weight(1)
     next(pairs[2])
     next(pairs[3])
+    row = jnp.sum(dots[...].T, axis=0, keepdims=True)
+    gz_out[0:1, :] = row[:, 0:128]
+    gz_out[1:2, :] = jnp.concatenate([row[:, 128:192], jnp.zeros((1, 64), F32)], axis=1)
+    gz_out[2:8, :] = jnp.zeros((6, T), F32)
+    for q in range(8):
+        go(gz_out, gz.at[e * 4 + b], gz_s.at[q], gz_r.at[e * 4 + b], holder(q))
+
+    weight(1)
     weight(2)
     ones = jnp.ones((16, 8 * T), BF16)
     bg_ref[...] = jnp.dot(ones, pg[...].reshape(8 * T, K), preferred_element_type=F32)[0:1, :].reshape(K)
     stores[5].start()
-    next(pairs[2])
-    next(pairs[3])
-
-    for half in (0, 1):
-        gz_out[half:half + 1, :] = jnp.sum(dots[half * T:(half + 1) * T, :].T, axis=0, keepdims=True)
-    gz_out[2:8, :] = jnp.zeros((6, T), F32)
-    for q in range(8):
-        go(gz_out, gz.at[e * 4 + b], gz_s.at[q], gz_r.at[e * 4 + b], holder(q))
 
     first = jnp.sum(stat2[:, 0, :], axis=0, keepdims=True) / D
     second = jnp.sum(stat2[:, 1, :], axis=0, keepdims=True) / D
+    total = jnp.zeros((F, T), F32)
     for n in range(4):
-        arrived(home_in.at[n * S:(n + 1) * S], hm_s.at[0], hm_r.at[n])
-    g = home_in[...] * gaint[...]
+        arrived(home_in.at[n], hm_s.at[0], hm_r.at[n])
+        total = total + home_in[n].astype(F32)
+    g = total * gaint[...]
     xg_ref[...] = (rstd * (g - first - normt[...] * second)).astype(BF16)
     stores[1].start()
     for n in range(8):
@@ -469,8 +454,8 @@
         vmem((8, K, T), BF16), vmem((8, K, T), BF16), vmem((8, T, K), F32), vmem((T, T), F32), vmem((8, T, K), BF16),
         vmem((8 * G, ROWS, K), BF16), vmem((8 * G, ROWS, K), BF16),
         vmem((4, K, T), BF16), vmem((4, K, T), BF16),
-        vmem((12, F, T), BF16), vmem((12, F, T), BF16), vmem((12, S, T), BF16), vmem((12, S, T), BF16),
-        vmem((4, S, T), F32), vmem((F, T), F32), vmem((2 * T, T), F32), vmem((4, K, T), F32),
+        vmem((12, F, T), BF16), vmem((12, F, T), BF16),
+        vmem((4, F, T), BF16), vmem((4, F, T), BF16), vmem((F, T), F32), vmem((4, K, T), F32),
         vmem((8, 1, K), F32), vmem((8, T), F32), vmem((8, 8, T), F32),
         vmem((T, K), BF16), vmem((F, T), BF16), vmem((K, K), F32), vmem((K,), F32), vmem((1, F), F32),
     ]
@@ -478,7 +463,7 @@
         sems(5), sems(7), sems(7), sems(7), sems(7), sems(7), sems(), sems(), sems(3), sems(3), sems(12), sems(12),
         sems(4), sems(4), sems(7), sems(7), sems(7), sems(7), sems(8), sems(8),
         sems(8 * G), sems(8 * G), sems(8 * G), sems(8 * G),
-        sems(4), sems(4), sems(12), sems(12), sems(12), sems(12), sems(4), sems(4),
+        sems(4), sems(4), sems(12), sems(12), sems(4), sems(4),
     ]
     anywhere = pl.BlockSpec(memory_space=pl.ANY)
     shapes = [

time: 89.9 us -> 87.2 us (0.970)
  Pallas kernels: 88.4 us -> 85.2 us
    pallas_call x1, Pallas kernels: 85.7 us -> 82.5 us  [body(): pl.pallas_call(kernel, out_shape=shapes, in_specs=[pl.BlockSpec(memory_sp...]
where the time goes in v4:
time: 87.2 us; the launch traced here: 85.9 us
  Pallas kernels  85.2 us (98%)
    pallas_call x1, Pallas kernels, body(): pl.pallas_call(kernel, out_shape=shapes, in_specs=[pl.BlockSpec(memory_sp...  82.5 us
    pallas_call x1, Pallas kernels, body(): pl.pallas_call(store, out_shape=shapes, in_specs=[anywhere] * 5, out_spec...  2.71 us

profile of v4, /device:TPU:1, one launch (start us, length us, event | category | flops | bytes accessed | tf_op | source)
XLA Modules:
  0.0 85.9 jit_solution(940647224408549502)
XLA Ops:
  0.6 82.5 %mlp_up.1 = (bf16[128,768]{1,0:T(8,128)(2,1)}, bf16[192,128]{1,0:T(8,128)(2,1)}, f32[768,768]{1,0:T(8,128)}, f32[768]{0:T(1024)}, f32[1,192]{1,0:T(1,128)}) custom-call(bf16[192,128]{1,0:T(8,128)(2,1)} %bitcast.4, f32[1,192]{1,0:T(1,128)} %bitcast.5, bf16[768,768]{1,0:T(8,128)(2,1)} %w_hbm.1, f32[768]{0:T(1024)} %bias_hbm.1, bf16[128,768]{1,0:T(8,128)(2,1)} %cot_hbm.1), custom_call_target="tpu_custom_call" | custom-call | tf_op jit(solution)/shard_map/mlp_up/pallas_call | solution.py:476
  83.2 2.7 %store.1 = (bf16[128,768]{1,0:T(8,128)(2,1)}, bf16[192,128]{1,0:T(8,128)(2,1)}, f32[768,768]{1,0:T(8,128)}, f32[768]{0:T(1024)}, f32[1,192]{1,0:T(1,128)}) custom-call(bf16[128,768]{1,0:T(8,128)(2,1)} %get-tuple-element.15.refs_0_, bf16[192,128]{1,0:T(8,128)(2,1)} %get-tuple-element.16.refs_1_, f32[768,768]{1,0:T(8,128)} %get-tuple-element.17.refs_2_, ...), custom_call_target="tpu_custom_call" | custom-call | tf_op jit(solution)/shard_map/store/pallas_call | solution.py:487

commit v5 on v4

--- a/solution.py
+++ b/solution.py
@@ -391,12 +391,14 @@
     row = jnp.sum(dots[...].T, axis=0, keepdims=True)
     gz_out[0:1, :] = row[:, 0:128]
     gz_out[1:2, :] = jnp.concatenate([row[:, 128:192], jnp.zeros((1, 64), F32)], axis=1)
-    gz_out[2:8, :] = jnp.zeros((6, T), F32)
     for q in range(8):
-        go(gz_out, gz.at[e * 4 + b], gz_s.at[q], gz_r.at[e * 4 + b], holder(q))
+        go(gz_out.at[0:2], gz.at[e * 4 + b, 0:2], gz_s.at[q], gz_r.at[e * 4 + b], holder(q))
 
     weight(1)
     weight(2)
+    for copy in pending[:-13]:
+        copy.wait_send()
+    del pending[:-13]
     ones = jnp.ones((16, 8 * T), BF16)
     bg_ref[...] = jnp.dot(ones, pg[...].reshape(8 * T, K), preferred_element_type=F32)[0:1, :].reshape(K)
     stores[5].start()
@@ -411,8 +413,8 @@
     xg_ref[...] = (rstd * (g - first - normt[...] * second)).astype(BF16)
     stores[1].start()
     for n in range(8):
-        arrived(gz.at[n], gz_s.at[0], gz_r.at[n])
-    row = jnp.sum(gz[...], axis=0)
+        arrived(gz.at[n, 0:2], gz_s.at[0], gz_r.at[n])
+    row = jnp.sum(gz[:, 0:2, :], axis=0)
     gg_ref[...] = jnp.concatenate([row[0:1, :], row[1:2, 0:64]], axis=1)
     stores[6].start()
 

time: 87.2 us -> 86.9 us (level)
  no operation moved by 1% of the time
where the time goes in v5:
time: 86.9 us; the launch traced here: 85.6 us
  Pallas kernels  84.9 us (98%)
    pallas_call x1, Pallas kernels, body(): pl.pallas_call(kernel, out_shape=shapes, in_specs=[pl.BlockSpec(memory_sp...  82.2 us
    pallas_call x1, Pallas kernels, body(): pl.pallas_call(store, out_shape=shapes, in_specs=[anywhere] * 5, out_spec...  2.71 us

profile of v5, /device:TPU:1, one launch (start us, length us, event | category | flops | bytes accessed | tf_op | source)
XLA Modules:
  0.0 85.6 jit_solution(9477313319160131601)
XLA Ops:
  0.6 82.2 %mlp_up.1 = (bf16[128,768]{1,0:T(8,128)(2,1)}, bf16[192,128]{1,0:T(8,128)(2,1)}, f32[768,768]{1,0:T(8,128)}, f32[768]{0:T(1024)}, f32[1,192]{1,0:T(1,128)}) custom-call(bf16[192,128]{1,0:T(8,128)(2,1)} %bitcast.4, f32[1,192]{1,0:T(1,128)} %bitcast.5, bf16[768,768]{1,0:T(8,128)(2,1)} %w_hbm.1, f32[768]{0:T(1024)} %bias_hbm.1, bf16[128,768]{1,0:T(8,128)(2,1)} %cot_hbm.1), custom_call_target="tpu_custom_call" | custom-call | tf_op jit(solution)/shard_map/mlp_up/pallas_call | solution.py:478
  82.9 2.7 %store.1 = (bf16[128,768]{1,0:T(8,128)(2,1)}, bf16[192,128]{1,0:T(8,128)(2,1)}, f32[768,768]{1,0:T(8,128)}, f32[768]{0:T(1024)}, f32[1,192]{1,0:T(1,128)}) custom-call(bf16[128,768]{1,0:T(8,128)(2,1)} %get-tuple-element.15.refs_0_, bf16[192,128]{1,0:T(8,128)(2,1)} %get-tuple-element.16.refs_1_, f32[768,768]{1,0:T(8,128)} %get-tuple-element.17.refs_2_, ...), custom_call_target="tpu_custom_call" | custom-call | tf_op jit(solution)/shard_map/store/pallas_call | solution.py:489

commit v6 on v5

--- a/solution.py
+++ b/solution.py
@@ -91,10 +91,10 @@
     def holder(q):
         return (q, 4 * r + my_k)
 
-    peers = [zpeer(j) for j in range(1, 8)]
-    peers += [apeer(j) for j in (1, 2, 3)] + [bpeer(j) for j in (1, 2, 3)] + [core]
-    peers += [holder(q) for q in range(8)]
+    peers = [holder((r + j) % 8) for j in (4, 3, 5, 2, 6, 1, 7, 0)]
     peers += [gatherer(c % 4, bb, ee) for bb in range(4) for ee in range(2)]
+    peers += [zpeer(j) for j in (4, 3, 5, 2, 6, 1, 7)]
+    peers += [apeer(j) for j in (2, 1, 3)] + [bpeer(j) for j in (2, 1, 3)] + [core]
     barrier = pltpu.get_barrier_semaphore()
     for peer in peers:
         pl.semaphore_signal(barrier, inc=1, device_id=peer, device_id_type=MESH)
@@ -204,6 +204,14 @@
         gaincol[k * F:(k + 1) * F, :] = jnp.broadcast_to(grow, (T, F)).T
         grows.append(split3(grow))
     loads[2].wait()
+    gaint[...] = jnp.broadcast_to(gain_ref[...], (T, F)).T
+    normt[...] = (xt - mean) * rstd
+    wbar = jnp.zeros((8, K), F32)
+    for k in range(4):
+        wbar += jnp.dot(grows[k], w_ref[k * F:(k + 1) * F, :], preferred_element_type=F32)
+    wz[r] = jnp.sum(wbar, axis=0, keepdims=True)
+    for j in range(1, 8):
+        go(wz.at[r], wz.at[r], wz_s.at[j - 1], wz_r.at[j - 1], zpeer(j))
     for j in range(1, 8):
         arrived(zstat.at[(r + 8 - j) % 8], zs_s.at[j - 1], zs_r.at[j - 1])
     for j in (0, 1, 3, 2):
@@ -271,14 +279,6 @@
     lax.fori_loop(3, 8, product, 0)
     for g in range(G):
         rs_step(1, g, (g % 2,))
-    gaint[...] = jnp.broadcast_to(gain_ref[...], (T, F)).T
-    normt[...] = (xt - mean) * rstd
-    wbar = jnp.zeros((8, K), F32)
-    for k in range(4):
-        wbar += jnp.dot(grows[k], w_ref[k * F:(k + 1) * F, :], preferred_element_type=F32)
-    wz[r] = jnp.sum(wbar, axis=0, keepdims=True)
-    for j in range(1, 8):
-        go(wz.at[r], wz.at[r], wz_s.at[j - 1], wz_r.at[j - 1], zpeer(j))
     for s in (2, 3):
         for g in range(G):
             rs_step(s, g, (g % 2, 1 - g % 2))
@@ -427,10 +427,11 @@
     ins, outs, held = refs[:5], refs[5:10], refs[10:15]
     in_sem, out_sem = refs[15:]
     rows = K // 8
-    parts = [(ins[i], held[i], outs[i]) for i in (0, 1, 3, 4)]
+    parts = []
     for i in range(8):
         at = pl.ds(i * rows, rows)
         parts.append((ins[2].at[at], held[2].at[at], outs[2].at[at]))
+    parts += [(ins[i], held[i], outs[i]) for i in (0, 1, 3, 4)]
     loads = [pltpu.make_async_copy(src, mid, in_sem.at[i]) for i, (src, mid, _) in enumerate(parts)]
     stores = [pltpu.make_async_copy(mid, dst, out_sem.at[i]) for i, (_, mid, dst) in enumerate(parts)]
     for load in loads:

time: 86.9 us -> 87 us (level)
  no operation moved by 1% of the time
where the time goes in v6:
time: 87 us; the launch traced here: 86.2 us
  Pallas kernels  85.6 us (98%)
    pallas_call x1, Pallas kernels, body(): pl.pallas_call(kernel, out_shape=shapes, in_specs=[pl.BlockSpec(memory_sp...  83 us
    pallas_call x1, Pallas kernels, body(): pl.pallas_call(store, out_shape=shapes, in_specs=[anywhere] * 5, out_spec...  2.64 us

profile of v6, /device:TPU:1, one launch (start us, length us, event | category | flops | bytes accessed | tf_op | source)
XLA Modules:
  0.0 86.2 jit_solution(13514816455327247123)
XLA Ops:
  0.6 83.0 %mlp_up.1 = (bf16[128,768]{1,0:T(8,128)(2,1)}, bf16[192,128]{1,0:T(8,128)(2,1)}, f32[768,768]{1,0:T(8,128)}, f32[768]{0:T(1024)}, f32[1,192]{1,0:T(1,128)}) custom-call(bf16[192,128]{1,0:T(8,128)(2,1)} %bitcast.4, f32[1,192]{1,0:T(1,128)} %bitcast.5, bf16[768,768]{1,0:T(8,128)(2,1)} %w_hbm.1, f32[768]{0:T(1024)} %bias_hbm.1, bf16[128,768]{1,0:T(8,128)(2,1)} %cot_hbm.1), custom_call_target="tpu_custom_call" | custom-call | tf_op jit(solution)/shard_map/mlp_up/pallas_call | solution.py:479
  83.6 2.6 %store.1 = (bf16[128,768]{1,0:T(8,128)(2,1)}, bf16[192,128]{1,0:T(8,128)(2,1)}, f32[768,768]{1,0:T(8,128)}, f32[768]{0:T(1024)}, f32[1,192]{1,0:T(1,128)}) custom-call(bf16[128,768]{1,0:T(8,128)(2,1)} %get-tuple-element.15.refs_0_, bf16[192,128]{1,0:T(8,128)(2,1)} %get-tuple-element.16.refs_1_, f32[768,768]{1,0:T(8,128)} %get-tuple-element.17.refs_2_, ...), custom_call_target="tpu_custom_call" | custom-call | tf_op jit(solution)/shard_map/store/pallas_call | solution.py:490

commit v7 on v5

--- a/solution.py
+++ b/solution.py
@@ -322,10 +322,15 @@
     def pair(p, even, odd):
         q = (r + 8 + (1 - swap) * even + swap * odd) % 8
         q_other = (r + 8 + (1 - swap) * odd + swap * even) % 8
-        both = dot_nt(w_ref[...], jnp.concatenate([pg[q_other], pg[q]], axis=0))
-        ce_out[p] = both[:, :T].astype(BF16)
-        go(ce_out.at[p], ce_in.at[p], ce_s.at[p], ce_r.at[p], core)
-        own[p] = both[:, T:]
+        if p == 3:
+            ce_out[p] = dot_nt(w_ref[...], pg[q_other]).astype(BF16)
+            go(ce_out.at[p], ce_in.at[p], ce_s.at[p], ce_r.at[p], core)
+            own[p] = dot_nt(w_ref[...], pg[q])
+        else:
+            both = dot_nt(w_ref[...], jnp.concatenate([pg[q_other], pg[q]], axis=0))
+            ce_out[p] = both[:, :T].astype(BF16)
+            go(ce_out.at[p], ce_in.at[p], ce_s.at[p], ce_r.at[p], core)
+            own[p] = both[:, T:]
         yield
         arrived(ce_in.at[p], ce_s.at[p], ce_r.at[p])
         for j in (2, 1, 3):

time: 86.9 us -> 87.2 us (level)
  no operation moved by 1% of the time
where the time goes in v7:
time: 87.2 us; the launch traced here: 86 us
  Pallas kernels  85.3 us (98%)
    pallas_call x1, Pallas kernels, body(): pl.pallas_call(kernel, out_shape=shapes, in_specs=[pl.BlockSpec(memory_sp...  82.6 us
    pallas_call x1, Pallas kernels, body(): pl.pallas_call(store, out_shape=shapes, in_specs=[anywhere] * 5, out_spec...  2.71 us

profile of v7, /device:TPU:1, one launch (start us, length us, event | category | flops | bytes accessed | tf_op | source)
XLA Modules:
  0.0 86.0 jit_solution(1409266122978923178)
XLA Ops:
  0.6 82.6 %mlp_up.1 = (bf16[128,768]{1,0:T(8,128)(2,1)}, bf16[192,128]{1,0:T(8,128)(2,1)}, f32[768,768]{1,0:T(8,128)}, f32[768]{0:T(1024)}, f32[1,192]{1,0:T(1,128)}) custom-call(bf16[192,128]{1,0:T(8,128)(2,1)} %bitcast.4, f32[1,192]{1,0:T(1,128)} %bitcast.5, bf16[768,768]{1,0:T(8,128)(2,1)} %w_hbm.1, f32[768]{0:T(1024)} %bias_hbm.1, bf16[128,768]{1,0:T(8,128)(2,1)} %cot_hbm.1), custom_call_target="tpu_custom_call" | custom-call | tf_op jit(solution)/shard_map/mlp_up/pallas_call | solution.py:483
  83.3 2.7 %store.1 = (bf16[128,768]{1,0:T(8,128)(2,1)}, bf16[192,128]{1,0:T(8,128)(2,1)}, f32[768,768]{1,0:T(8,128)}, f32[768]{0:T(1024)}, f32[1,192]{1,0:T(1,128)}) custom-call(bf16[128,768]{1,0:T(8,128)(2,1)} %get-tuple-element.15.refs_0_, bf16[192,128]{1,0:T(8,128)(2,1)} %get-tuple-element.16.refs_1_, f32[768,768]{1,0:T(8,128)} %get-tuple-element.17.refs_2_, ...), custom_call_target="tpu_custom_call" | custom-call | tf_op jit(solution)/shard_map/store/pallas_call | solution.py:494
